TPU v7x, 512 devices: a whole 4x4x16 slice. The times are simulated.
512 devices in a mesh: blk: 128 (over z, y, core), term: 4 (over x).
Axes of the slice: x: 4, y: 4, z: 16, core: 2. Of those that a mesh axis runs over, the one named last changes fastest.
Arguments:
- psi: bfloat16 [512, 256, 256], P('blk'), may hold values from -6 to 6
- left_env: bfloat16 [8, 2, 256, 256], P('term'), may hold values from -0.25 to 0.25
- right_env: bfloat16 [8, 2, 256, 256], P('term'), may hold values from -0.25 to 0.25
- connect: int32 [8, 512], P('term'), may hold values from 0 to 511, each once within a row
- qclass: int32 [512], replicated, may hold values from 0 to 1
- sector_dims: int32 [512], replicated, may hold values from 64 to 256, as said below
Outputs:
- sigma_one: bfloat16 [512, 256, 256], P('blk')
- sigma_two: bfloat16 [512, 256, 256], P('term', 'blk')
Inputs may be any that keep to these rules, and one draw needn't show every extreme that they name: `sector_dims`: some sector has dimension exactly 256 and some exactly 64. `connect`: each row is a permutation of the sectors.
All inputs are finite; a program needn't handle non-finite values.
Results may differ from a plain program's by a relative error of at most 0.0065.
Values may be sent and summed in bfloat16 or wider, within the bound.
No kernel may reach another device: no remote copies, remote signals or barrier semaphores. Data moves between devices by JAX's collectives and lax.ppermute only.
A program may use at most 64 MiB of HBM per device.

v0:
```python
import jax
import jax.numpy as jnp
from jax import lax
from jax.sharding import PartitionSpec as P


def on_device(psi, left_env, right_env, connect, qclass, sector_dims):
    nblk = lax.axis_size("blk")
    sec_dev = psi.shape[0]
    width = psi.shape[1]
    band = width // nblk
    nsec = qclass.shape[0]
    terms_here = left_env.shape[0]
    classes = left_env.shape[1]
    blk_index = lax.axis_index("blk")
    first = blk_index * sec_dev
    q_local = lax.dynamic_slice_in_dim(qclass, first, sec_dev)
    d_local = lax.dynamic_slice_in_dim(sector_dims, first, sec_dev)
    line = jnp.arange(width, dtype=jnp.int32)
    sector_mask = (line[None, :, None] < d_local[:, None, None]) & (
        line[None, None, :] < d_local[:, None, None]
    )
    global_rows = blk_index * band + jnp.arange(band, dtype=jnp.int32)
    row_mask = (global_rows[None, :, None] < sector_dims[:, None, None]) & (
        line[None, None, :] < sector_dims[:, None, None]
    )
    left_pick = jnp.take(left_env, q_local, axis=1)

    def partial_terms(vec):
        masked = jnp.where(sector_mask, vec, jnp.zeros_like(vec))
        contracted = jnp.einsum(
            "tsij,sjk->tsik", left_pick, masked, preferred_element_type=jnp.float32
        ).astype(jnp.bfloat16)
        pieces = contracted.reshape(terms_here, sec_dev, nblk, band, width)
        moved = lax.all_to_all(pieces, "blk", split_axis=2, concat_axis=1, tiled=True)
        moved = moved.reshape(terms_here, nsec, band, width)
        total = jnp.zeros((nsec, band, width), jnp.float32)
        for which in range(terms_here):
            source = jnp.take(moved[which], connect[which], axis=0).reshape(nsec * band, width)
            for level in range(classes):
                image = jnp.einsum(
                    "rk,lk->rl", source, right_env[which, level], preferred_element_type=jnp.float32
                )
                image = image.reshape(nsec, band, width)
                chosen = (qclass == level)[:, None, None]
                total = total + jnp.where(chosen, image, 0.0)
        return jnp.where(row_mask, total, 0.0)

    first_total = partial_terms(psi)
    summed = lax.psum(first_total, "term").astype(jnp.bfloat16)
    bands = summed.reshape(nblk, sec_dev, band, width)
    sectors = lax.all_to_all(bands, "blk", split_axis=0, concat_axis=2, tiled=True)
    sigma_one = sectors.reshape(sec_dev, width, width)
    second_total = partial_terms(sigma_one)
    sigma_two = lax.psum_scatter(second_total, "term", scatter_dimension=0, tiled=True).astype(
        jnp.bfloat16
    )
    return (sigma_one, sigma_two)


def solution(mesh):
    placed = (
        P("blk", None, None),
        P("term", None, None, None),
        P("term", None, None, None),
        P("term", None),
        P(),
        P(),
    )
    return jax.shard_map(
        on_device,
        mesh=mesh,
        in_specs=placed,
        out_specs=(P("blk", None, None), P("term", "blk", None)),
        check_vma=False,
    )
```

profile of v0, /device:TPU:32, one launch (start us, length us, event | category | flops | bytes accessed | tf_op | source)
XLA Modules:
  0.0 288.9 jit_solution(4924389895817824429)
XLA Ops:
  7.2 0.8 dynamic_slice.6
  8.1 0.8 compare_and_fusion.2
  8.9 0.6 gather_fusion
  9.5 1.0 copy-done.2
  10.5 0.5 fusion.8
  11.0 0.4 reshape.171
  11.5 1.7 copy.22
  13.2 19.3 %all-to-all-start = ((bf16[2,4,128,2,256]{4,3,1,0,2:T(2,128)(2,1)}), bf16[2,4,128,2,256]{4,3,1,0,2:T(2,128)(2,1)S(1)}, u32[]{:S(2)}, u32[]{:S(2)}) async-start(bf16[2,4,128,2,256]{4,3,1,0,2:T(2,128)(2,1)} %copy.22), calls=%async_computation | async-start | bytes 2097152 | tf_op jit(solution)/shard_map/all_to_all | solution.py:35
  32.9 55.0 %all-to-all-done = bf16[2,4,128,2,256]{4,3,1,0,2:T(2,128)(2,1)S(1)} async-done(((bf16[2,4,128,2,256]{4,3,1,0,2:T(2,128)(2,1)}), bf16[2,4,128,2,256]{4,3,1,0,2:T(2,128)(2,1)S(1)}, u32[]{:S(2)}, u32[]{:S(2)}) %all-to-all-start) | async-done | bytes 1048608 | tf_op jit(solution)/shard_map/all_to_all | solution.py:35
  88.0 1.5 fusion.51
  89.5 2.6 gather_fusion.2
  92.0 1.8 broadcast_select_fusion.2
  94.5 3.8 %gather_fusion.1 = bf16[512,2,256]{2,1,0:T(2,128)(2,1)} fusion(bf16[512,2,256]{2,1,0:T(2,128)(2,1)} %bitcast.78, s32[1024]{0:T(1024)S(1)} %pad_clamp_fusion.1), kind=kCustom, calls=%fused_computation.clone | custom fusion | bytes 1050624 | tf_op jit(solution)/shard_map/jit(_take)/gather | solution.py:39
  98.4 3.0 %broadcast_select_fusion.4 = bf16[512,2,256]{2,1,0:T(2,128)(2,1)S(1)} fusion(bf16[512,2,256]{2,1,0:T(2,128)(2,1)} %gather_fusion.1, pred[512]{0:T(512)(128)(4,1)S(1)} %compare_and_fusion.1), kind=kLoop, calls=%fused_computation.33 | loop fusion | flops 262144 | bytes 1049088 | tf_op jit(solution)/shard_map/jit(_take)/select_n | solution.py:39
  101.4 0.3 convolution_select_fusion.6
  101.7 1.6 fusion.3
  103.3 33.4 %all-reduce.1 = bf16[512,2,256]{2,0,1:T(8,128)(2,1)S(1)} all-reduce(f32[512,2,256]{2,0,1:T(8,128)} %fusion.3), channel_id=1, replica_groups=mesh['blk'=128,'term'=4] {'term'}, use_global_device_ids=true, to_apply=%region_0.0 | all-reduce | flops 262144 | bytes 1572864 | tf_op jit(solution)/shard_map/psum | solution.py:50
  137.1 39.9 %all_to_all.45 = bf16[128,4,2,256]{3,1,2,0:T(4,128)(2,1)S(1)} all-to-all(bf16[128,4,2,256]{3,1,2,0:T(4,128)(2,1)S(1)} %copy.27), channel_id=1, replica_groups=mesh['blk'=128,'term'=4] {'blk'}, dimensions={0} | all-to-all | bytes 1048576 | tf_op jit(solution)/shard_map/all_to_all | solution.py:52
  177.0 0.8 copy-done.4
  177.8 1.5 fusion.9
  179.3 1.5 reshape.174
  180.8 0.7 copy.29
  181.5 62.1 %all_to_all.46 = bf16[2,4,128,2,256]{4,3,1,0,2:T(2,128)(2,1)S(1)} all-to-all(bf16[2,4,128,2,256]{4,3,1,0,2:T(2,128)(2,1)S(1)} %copy.29), channel_id=1, replica_groups=mesh['blk'=128,'term'=4] {'blk'}, dimensions={2} | all-to-all | bytes 2097152 | tf_op jit(solution)/shard_map/all_to_all | solution.py:35
  243.6 1.5 fusion.50
  245.2 2.6 gather_fusion.4
  247.7 1.8 broadcast_select_fusion.1
  250.2 3.8 %gather_fusion.3 = bf16[512,2,256]{2,1,0:T(2,128)(2,1)} fusion(bf16[512,2,256]{2,1,0:T(2,128)(2,1)} %bitcast.77, s32[1024]{0:T(1024)S(1)} %pad_clamp_fusion.1), kind=kCustom, calls=%fused_computation.2.clone | custom fusion | bytes 1050624 | tf_op jit(solution)/shard_map/jit(_take)/gather | solution.py:39
  254.0 3.0 %broadcast_select_fusion.3 = bf16[512,2,256]{2,1,0:T(2,128)(2,1)S(1)} fusion(bf16[512,2,256]{2,1,0:T(2,128)(2,1)} %gather_fusion.3, pred[512]{0:T(512)(128)(4,1)S(1)} %compare_and_fusion.1), kind=kLoop, calls=%fused_computation.32 | loop fusion | flops 262144 | bytes 1049088 | tf_op jit(solution)/shard_map/jit(_take)/select_n | solution.py:39
  257.4 1.6 fusion.7
  258.9 21.3 %reduce-scatter.2.cloned.1.call-done = f32[128,2,256]{2,0,1:T(8,128)} async-done(((f32[512,2,256]{2,0,1:T(8,128)}), f32[128,2,256]{2,0,1:T(8,128)}) %reduce-scatter.2.cloned.1.call-update) | async-done | bytes 262160 | tf_op jit(solution)/shard_map/reduce_scatter | solution.py:55
  280.3 1.0 convert_element_type.23
  281.2 0.8 copy.35
  (39 shorter events, 2.5 us)
Async XLA Ops:
  7.2 1.7 copy-start
  8.9 1.6 copy-start.8
  9.5 1.0 copy-start.2
  13.2 19.4 %copy-start.6 = (s32[2,512]{1,0:T(2,128)S(1)}, s32[2,512]{1,0:T(2,128)}, u32[]{:S(2)}) copy-start(s32[2,512]{1,0:T(2,128)} %param.11) | copy-start | bytes 12292
  13.2 19.5 %copy-start.7 = (s32[512]{0:T(512)S(1)}, s32[512]{0:T(512)}, u32[]{:S(2)}) copy-start(s32[512]{0:T(512)} %param.12) | copy-start | bytes 6148
  13.2 19.5 %copy-start.5 = (s32[512]{0:T(512)S(1)}, s32[512]{0:T(512)}, u32[]{:S(2)}) copy-start(s32[512]{0:T(512)} %param.13) | copy-start | bytes 6148
  13.2 74.8 %all-to-all-start = ((bf16[2,4,128,2,256]{4,3,1,0,2:T(2,128)(2,1)}), bf16[2,4,128,2,256]{4,3,1,0,2:T(2,128)(2,1)S(1)}, u32[]{:S(2)}, u32[]{:S(2)}) async-start(bf16[2,4,128,2,256]{4,3,1,0,2:T(2,128)(2,1)} %copy.22), calls=%async_computation | async-start | bytes 2097152 | tf_op jit(solution)/shard_map/all_to_all | solution.py:35
  32.5 247.8 %reduce-scatter.2.cloned.1.call-start = ((), (), s32[]{:S(2)}) async-start(), calls=%async_computation.4 | async-start | bytes 1310720 | tf_op jit(solution)/shard_map/reduce_scatter | solution.py:55
  89.5 4.4 %copy-start.1 = (bf16[2,2,256,256]{3,2,1,0:T(8,128)(2,1)S(1)}, bf16[2,2,256,256]{3,2,1,0:T(8,128)(2,1)}, u32[]{:S(2)}) copy-start(bf16[2,2,256,256]{3,2,1,0:T(8,128)(2,1)} %param.10) | copy-start | bytes 1572868
  137.1 40.7 %copy-start.3 = (bf16[4,2,256,256]{3,2,1,0:T(8,128)(2,1)S(1)}, bf16[4,2,256,256]{3,2,1,0:T(8,128)(2,1)}, u32[]{:S(2)}) copy-start(bf16[4,2,256,256]{3,2,1,0:T(8,128)(2,1)} %copy-done.2) | copy-start | bytes 3145732
  177.0 0.8 copy-start.4
Sparse Core Ops, SparseCore 0:
  259.1 21.1 reduce-scatter.1
where the time goes:
time: 290 us; the launch traced here: 289 us
  blocking collectives  135 us (47%)
  waiting for transfers between devices  76.4 us (26%)
  local copies, waits for them, and re-layouts  24.5 us (8%)
  starting transfers between devices  19.3 us (7%)
  between operations  14.4 us (5%)
  other arithmetic  11.7 us (4%)
  matrix products  7.24 us (2%)
    all_to_all x1, blocking collectives, partial_terms(): lax.all_to_all(pieces, 'blk', split_axis=2, concat_axis=1, tiled=True)  62.1 us
    all_to_all x1, waiting for transfers between devices, partial_terms(): lax.all_to_all(pieces, 'blk', split_axis=2, concat_axis=1, tiled=True)  55 us
    all_to_all x1, blocking collectives, on_device(): lax.all_to_all(bands, 'blk', split_axis=0, concat_axis=2, tiled=True)  39.9 us
    psum x1, blocking collectives, on_device(): summed = lax.psum(first_total, 'term').astype(jnp.bfloat16)  33.4 us
    reduce_scatter x1, waiting for transfers between devices, on_device(): lax.psum_scatter(second_total, 'term', scatter_dimension=0, tiled=True)  21.3 us
    all_to_all x1, starting transfers between devices, partial_terms(): lax.all_to_all(pieces, 'blk', split_axis=2, concat_axis=1, tiled=True)  19.3 us
    gather x4, local copies, waits for them, and re-layouts, partial_terms(): jnp.take(moved[which], connect[which], axis=0).reshape(nsec * band, width)  12.7 us
    select_n x6, other arithmetic, partial_terms(): jnp.take(moved[which], connect[which], axis=0).reshape(nsec * band, width)  9.64 us
  transfers between devices with their start and end apart: 2, of which 2 were waited for; matrix products, arithmetic and copies ran while one was open for 0% of the time, Pallas kernels for 0%

commit v1 on v0

v1 whole, which is shorter than its diff:
```python
import jax
import jax.numpy as jnp
from jax import lax
from jax.experimental import pallas as pl
from jax.experimental.pallas import tpu as pltpu
from jax.sharding import PartitionSpec as P

LANES = 128


def pair_kernel(scalars, vec, left, right, order, out, wide):
    sec, width = vec.shape[0], vec.shape[1]
    terms, classes = left.shape[0], left.shape[1]
    half = width // 2
    pairs = terms * sec
    row = lax.broadcasted_iota(jnp.int32, (width, width), 0)
    col = lax.broadcasted_iota(jnp.int32, (width, width), 1)
    edge = jnp.maximum(row, col)
    for c in range(sec):
        masked = jnp.where(edge < scalars[sec + c], vec[c], jnp.zeros_like(vec[c]))
        for t in range(terms):
            contracted = jnp.dot(
                left[t, scalars[c]], masked, preferred_element_type=jnp.float32
            ).astype(jnp.bfloat16)
            sorted_rows = jnp.dot(
                order[...], contracted, preferred_element_type=jnp.float32
            ).astype(jnp.bfloat16)
            image = lax.dot_general(
                sorted_rows,
                right[t, scalars[2 * sec + t * sec + c]],
                (((1,), (1,)), ((), ())),
                preferred_element_type=jnp.float32,
            )
            pair = t * sec + c
            for j in range(wide.shape[0]):
                r, at = j // (width // LANES), j % (width // LANES) * LANES
                wide[j, pl.ds(pair, half, stride=pairs), :] = image[
                    r * half : (r + 1) * half, at : at + LANES
                ]
    for j in range(wide.shape[0]):
        out[:, j * LANES : (j + 1) * LANES] = wide[j].astype(jnp.bfloat16)


def pair_products(scalars, vec, left, right, order):
    terms, sec, width = left.shape[0], vec.shape[0], vec.shape[1]
    rows = terms * sec * width // 2
    vmem = pl.BlockSpec(memory_space=pltpu.VMEM)
    return pl.pallas_call(
        pair_kernel,
        out_shape=jax.ShapeDtypeStruct((rows, 2 * width), jnp.bfloat16),
        in_specs=[pl.BlockSpec(memory_space=pltpu.SMEM), vmem, vmem, vmem, vmem],
        out_specs=vmem,
        scratch_shapes=[pltpu.VMEM((2 * width // LANES, rows, LANES), jnp.float32)],
        compiler_params=pltpu.CompilerParams(vmem_limit_bytes=32 * 1024 * 1024),
        cost_estimate=pl.CostEstimate(
            flops=terms * sec * 3 * 2 * width**3, bytes_accessed=4 * 1024 * 1024, transcendentals=0
        ),
    )(scalars, vec, left, right, order)


def on_device(psi, left_env, right_env, connect, qclass, sector_dims):
    nblk = lax.axis_size("blk")
    nterm = lax.axis_size("term")
    sec_dev, width = psi.shape[0], psi.shape[1]
    band = width // nblk
    nsec = qclass.shape[0]
    terms = left_env.shape[0]
    pairs = terms * sec_dev
    blk = lax.axis_index("blk")
    first = blk * sec_dev

    mine = first + jnp.arange(sec_dev, dtype=jnp.int32)
    sectors = jnp.arange(nsec, dtype=jnp.int32)
    own = (sectors[None, :] == mine[:, None]).astype(jnp.int32)
    q_local = jnp.sum(own * qclass[None, :], axis=1)
    d_local = jnp.sum(own * sector_dims[None, :], axis=1)
    hit = (connect[:, None, :] == mine[None, :, None]).astype(jnp.int32)
    q_target = jnp.sum(hit * qclass[None, None, :], axis=2)
    scalars = jnp.concatenate([q_local, d_local, q_target.reshape(-1)])

    line = jnp.arange(width, dtype=jnp.int32)
    place = jnp.where(line < width // 2, 2 * line, 2 * line - width + 1)
    order = (place[:, None] == line[None, :]).astype(jnp.bfloat16)

    k = jnp.arange(nblk * pairs, dtype=jnp.int32)
    k_term = (k // sec_dev) % terms
    k_sector = (k // pairs) * sec_dev + k % sec_dev

    def routing(targets):
        wanted = jnp.zeros((nsec, k.shape[0]), jnp.int32)
        for t in range(terms):
            wanted = jnp.where(k_term[None, :] == t, targets[t][:, None], wanted)
        return (wanted == k_sector[None, :]).astype(jnp.bfloat16)

    def by_owner(a):
        return a.reshape(nblk, sec_dev).T.reshape(nsec)

    route_one = routing([by_owner(connect[t]) for t in range(terms)])
    route_two = routing([connect[t] for t in range(terms)])
    element = jnp.arange(band * width, dtype=jnp.int32)
    edge = jnp.maximum(blk * band + element // width, element % width)
    keep_one = edge[None, :] < by_owner(sector_dims)[:, None]
    keep_two = edge[None, :] < sector_dims[:, None]

    def product(vec, route, keep):
        sent = pair_products(scalars, vec, left_env, right_env, order)
        sent = sent.reshape(nblk, pairs, band * width)
        moved = lax.all_to_all(sent, "blk", split_axis=0, concat_axis=0, tiled=True)
        moved = moved.reshape(nblk * pairs, band * width)
        total = jnp.dot(route, moved, preferred_element_type=jnp.float32)
        total = jnp.where(keep, total, 0.0).astype(jnp.bfloat16)
        total = total.reshape(nterm, nsec // nterm, band * width)
        parts = lax.all_to_all(total, "term", split_axis=0, concat_axis=0, tiled=True)
        return jnp.sum(parts.astype(jnp.float32), axis=0).astype(jnp.bfloat16)

    one = product(psi, route_one, keep_one)
    one = one.reshape(nblk, band, width)
    one = lax.all_to_all(one, "blk", split_axis=0, concat_axis=0, tiled=True)
    one = one.reshape(1, width, width)
    sigma_one = lax.all_gather(one, "term", axis=0, tiled=True)
    two = product(sigma_one, route_two, keep_two)
    sigma_two = two.reshape(nsec // nterm, band, width)
    return (sigma_one, sigma_two)


def solution(mesh):
    placed = (
        P("blk", None, None),
        P("term", None, None, None),
        P("term", None, None, None),
        P("term", None),
        P(),
        P(),
    )
    return jax.shard_map(
        on_device,
        mesh=mesh,
        in_specs=placed,
        out_specs=(P("blk", None, None), P("term", "blk", None)),
        check_vma=False,
    )
```

time: 290 us -> 216 us (0.74)
  waiting for transfers between devices: 76.4 us -> 54.8 us
  local copies, waits for them, and re-layouts: 24.5 us -> 5.35 us
  between operations: 14.4 us -> 0.77 us
  blocking collectives: 135 us -> 125 us
  other arithmetic: 11.7 us -> 2.19 us
  Pallas kernels: 0 us -> 7.02 us
  matrix products: 7.24 us -> 1.52 us
    psum x1 -> x0, blocking collectives: 33.4 us -> none  [on_device(): summed = lax.psum(first_total, 'term').astype(jnp.bfloat16)]
    reduce_scatter x1 -> x0, waiting for transfers between devices: 21.3 us -> none  [on_device(): lax.psum_scatter(second_total, 'term', scatter_dimension=0, tiled=True)]
    gather x5 -> x0, local copies, waits for them, and re-layouts: 13.3 us -> none  [the longest x4 12.7 us: partial_terms(): jnp.take(moved[which], connect[which], axis=0).reshape(nsec * band, width)]
    all_gather x0 -> x1, blocking collectives: none -> 13.2 us  [on_device(): sigma_one = lax.all_gather(one, 'term', axis=0, tiled=True)]
    all_to_all x2 -> x4, blocking collectives: 102 us -> 112 us  [the longest x1 61.6 us: product(): moved = lax.all_to_all(sent, 'blk', split_axis=0, concat_axis=0, tiled=True)]
    select_n x6 -> x1, other arithmetic: 9.64 us -> 0.01 us  [on_device(): place = jnp.where(line < width // 2, 2 * line, 2 * line - width + 1)]
    pallas_call x0 -> x2, Pallas kernels: none -> 7.02 us  [pair_products(): pl.pallas_call(pair_kernel, out_shape=jax.ShapeDtypeStruct((rows, 2 * wid...]
    dot_general x10 -> x2, matrix products: 7.24 us -> 1.52 us  [product(): total = jnp.dot(route, moved, preferred_element_type=jnp.float32)]
  transfers between devices with their start and end apart: 2 -> 1, of which waited for: 2 -> 1; matrix products, arithmetic and copies ran while one was open for 0% -> 0% of each run, Pallas kernels for 0% -> 0%
where the time goes in v1:
time: 216 us
  blocking collectives  125 us (58%)
  waiting for transfers between devices  54.8 us (25%)
  starting transfers between devices  19.3 us (9%)
  Pallas kernels  7.02 us (3%)
  local copies, waits for them, and re-layouts  5.35 us (2%)
  other arithmetic  2.19 us (1%)
    all_to_all x1, blocking collectives, product(): moved = lax.all_to_all(sent, 'blk', split_axis=0, concat_axis=0, tiled=True)  61.6 us
    all_to_all x1, waiting for transfers between devices, product(): moved = lax.all_to_all(sent, 'blk', split_axis=0, concat_axis=0, tiled=True)  54.8 us
    all_to_all x2, blocking collectives, product(): lax.all_to_all(total, 'term', split_axis=0, concat_axis=0, tiled=True)  26.7 us
    all_to_all x1, blocking collectives, on_device(): one = lax.all_to_all(one, 'blk', split_axis=0, concat_axis=0, tiled=True)  23.5 us
    all_to_all x1, starting transfers between devices, product(): moved = lax.all_to_all(sent, 'blk', split_axis=0, concat_axis=0, tiled=True)  19.3 us
    all_gather x1, blocking collectives, on_device(): sigma_one = lax.all_gather(one, 'term', axis=0, tiled=True)  13.2 us
    pallas_call x2, Pallas kernels, pair_products(): pl.pallas_call(pair_kernel, out_shape=jax.ShapeDtypeStruct((rows, 2 * wid...  7.02 us
  transfers between devices with their start and end apart: 1, of which 1 were waited for; matrix products, arithmetic and copies ran while one was open for 0% of the time, Pallas kernels for 0%

profile of v1, /device:TPU:32, one launch (start us, length us, event | category | flops | bytes accessed | tf_op | source)
XLA Modules:
  0.0 215.9 jit_solution(2373633482306720985)
XLA Ops:
  0.7 0.9 select_reduce_fusion
  1.6 0.1 reshape.136
  1.6 0.9 select_reduce_fusion.2
  2.5 0.1 fusion.20.order
  2.7 0.1 pad_add_fusion.scalars
  2.7 1.0 copy-done
  3.8 1.0 copy-done.1
  4.8 1.0 copy-done.3
  5.9 4.0 %shard_map.77 = bf16[1024,512]{1,0:T(8,128)(2,1)} custom-call(s32[16]{0:T(128)S(1)} %pad_add_fusion.scalars, bf16[4,256,256]{2,1,0:T(8,128)(2,1)S(1)} %copy-done, bf16[2,2,256,256]{3,2,1,0:T(8,128)(2,1)S(1)} %copy-done.1, bf16[2,2,256,256]{3,2,1,0:T(8,128)(2,1)S(1)} %copy-done.3, bf16[256,256]{1,0:T(8,128)(2,1)S(1)} %fusion.20.order), custom_call_target="tpu_custom_call" | custom-call | flops 805306368 | bytes 4194304 | tf_op jit(solution)/shard_map/pallas_call | solution.py:48
  9.9 19.3 %all-to-all-start = ((bf16[128,8,512]{2,1,0:T(8,128)(2,1)}), bf16[128,8,512]{2,1,0:T(8,128)(2,1)S(1)}, u32[]{:S(2)}, u32[]{:S(2)}) async-start(bf16[128,8,512]{2,1,0:T(8,128)(2,1)} %bitcast.6), calls=%async_computation | async-start | bytes 2097152 | tf_op jit(solution)/shard_map/all_to_all | solution.py:108
  29.2 0.0 copy-done.6
  29.2 0.1 reshape.135
  29.3 0.1 reshape_squeeze.6
  29.5 0.1 copy.15
  29.5 0.1 reshape_squeeze.7
  29.6 0.1 copy.16
  29.7 0.1 copy.14
  29.8 54.8 %all-to-all-done = bf16[128,8,512]{2,1,0:T(8,128)(2,1)S(1)} async-done(((bf16[128,8,512]{2,1,0:T(8,128)(2,1)}), bf16[128,8,512]{2,1,0:T(8,128)(2,1)S(1)}, u32[]{:S(2)}, u32[]{:S(2)}) %all-to-all-start) | async-done | bytes 1048608 | tf_op jit(solution)/shard_map/all_to_all | solution.py:108
  84.6 0.8 fusion.5
  85.4 14.0 %all_to_all.25 = bf16[4,128,512]{2,1,0:T(8,128)(2,1)S(1)} all-to-all(bf16[4,128,512]{2,1,0:T(8,128)(2,1)S(1)} %bitcast.20), channel_id=1, replica_groups=mesh['blk'=128,'term'=4] {'term'}, dimensions={0} | all-to-all | bytes 1048576 | tf_op jit(solution)/shard_map/all_to_all | solution.py:113
  99.5 0.1 reduce_sum.54
  99.6 23.5 %all_to_all.26 = bf16[128,2,256]{2,1,0:T(2,128)(2,1)S(1)} all-to-all(bf16[128,2,256]{2,1,0:T(2,128)(2,1)S(1)} %reshape.140), channel_id=1, replica_groups=mesh['blk'=128,'term'=4] {'blk'}, dimensions={0} | all-to-all | bytes 262144 | tf_op jit(solution)/shard_map/all_to_all | solution.py:118
  123.1 0.1 reshape.141
  123.1 13.2 %all_gather.3.vec = bf16[4,256,256]{2,1,0:T(8,128)(2,1)S(1)} all-gather(bf16[1,256,256]{2,1,0:T(8,128)(2,1)S(1)} %reshape.141), channel_id=1, replica_groups=mesh['blk'=128,'term'=4] {'term'}, dimensions={0}, use_global_device_ids=true | all-gather | bytes 655360 | tf_op jit(solution)/shard_map/all_gather | solution.py:120
  136.3 0.0 copy-done.2
  136.3 3.0 %shard_map.78 = bf16[1024,512]{1,0:T(8,128)(2,1)S(1)} custom-call(s32[16]{0:T(128)S(1)} %pad_add_fusion.scalars, bf16[4,256,256]{2,1,0:T(8,128)(2,1)S(1)} %all_gather.3.vec, bf16[2,2,256,256]{3,2,1,0:T(8,128)(2,1)S(1)} %copy-done.2, bf16[2,2,256,256]{3,2,1,0:T(8,128)(2,1)S(1)} %copy-done.4, bf16[256,256]{1,0:T(8,128)(2,1)S(1)} %fusion.20.order), custom_call_target="tpu_custom_call" | custom-call | flops 805306368 | bytes 4194304 | tf_op jit(solution)/shard_map/pallas_call | solution.py:48
  139.4 61.6 %all_to_all.27 = bf16[128,8,512]{2,1,0:T(8,128)(2,1)S(1)} all-to-all(bf16[128,8,512]{2,1,0:T(8,128)(2,1)S(1)} %bitcast.18), channel_id=1, replica_groups=mesh['blk'=128,'term'=4] {'blk'}, dimensions={0} | all-to-all | bytes 2097152 | tf_op jit(solution)/shard_map/all_to_all | solution.py:108
  200.9 0.8 fusion.3
  201.7 12.6 %all_to_all.28 = bf16[4,128,512]{2,1,0:T(8,128)(2,1)S(1)} all-to-all(bf16[4,128,512]{2,1,0:T(8,128)(2,1)S(1)} %bitcast.19), channel_id=1, replica_groups=mesh['blk'=128,'term'=4] {'term'}, dimensions={0} | all-to-all | bytes 1048576 | tf_op jit(solution)/shard_map/all_to_all | solution.py:113
  214.3 0.1 reduce_sum.55
  214.4 0.7 reshape.145
  215.1 0.8 copy.18
  (16 shorter events, 0.1 us)
Async XLA Ops:
  2.7 1.0 copy-start
  3.8 1.0 copy-start.1
  4.8 1.0 copy-start.3
  9.9 19.3 %copy-start.6 = (s32[512]{0:T(512)S(1)}, s32[512]{0:T(512)}, u32[]{:S(2)}) copy-start(s32[512]{0:T(512)} %param.11) | copy-start | bytes 6148
  9.9 19.4 %copy-start.5 = (s32[2,512]{1,0:T(2,128)S(1)}, s32[2,512]{1,0:T(2,128)}, u32[]{:S(2)}) copy-start(s32[2,512]{1,0:T(2,128)} %param.9) | copy-start | bytes 12292
  9.9 74.8 %all-to-all-start = ((bf16[128,8,512]{2,1,0:T(8,128)(2,1)}), bf16[128,8,512]{2,1,0:T(8,128)(2,1)S(1)}, u32[]{:S(2)}, u32[]{:S(2)}) async-start(bf16[128,8,512]{2,1,0:T(8,128)(2,1)} %bitcast.6), calls=%async_computation | async-start | bytes 2097152 | tf_op jit(solution)/shard_map/all_to_all | solution.py:108
  99.5 36.9 %copy-start.2 = (bf16[2,2,256,256]{3,2,1,0:T(8,128)(2,1)S(1)}, bf16[2,2,256,256]{3,2,1,0:T(8,128)(2,1)}, u32[]{:S(2)}) copy-start(bf16[2,2,256,256]{3,2,1,0:T(8,128)(2,1)} %left.3) | copy-start | bytes 1572868
  99.5 36.9 %copy-start.4 = (bf16[2,2,256,256]{3,2,1,0:T(8,128)(2,1)S(1)}, bf16[2,2,256,256]{3,2,1,0:T(8,128)(2,1)}, u32[]{:S(2)}) copy-start(bf16[2,2,256,256]{3,2,1,0:T(8,128)(2,1)} %right.3) | copy-start | bytes 1572868

commit v2 on v0

v2 whole, which is shorter than its diff:
```python
import functools

import jax
import jax.numpy as jnp
from jax import lax
from jax.experimental import pallas as pl
from jax.experimental.pallas import tpu as pltpu
from jax.sharding import PartitionSpec as P

LANES = 128
CODE_ROWS = 16
CODE_BASE = 16
F32, BF16 = jnp.float32, jnp.bfloat16
NT = (((1,), (1,)), ((), ()))


def matmul(a, b):
    return jnp.dot(a, b, preferred_element_type=F32)


def matmul_nt(a, b):
    return lax.dot_general(a, b, NT, preferred_element_type=F32)


def iota(shape, dim):
    return lax.broadcasted_iota(jnp.int32, shape, dim)


def split_order(width):
    half = width // 2
    line = iota((width, width), 0)
    place = jnp.where(line < half, 2 * line, 2 * line - width + 1)
    return (place == iota((width, width), 1)).astype(F32).astype(BF16)


def source_kernel(
    psi_hbm, left_hbm, right_hbm, conn_hbm, qclass_hbm, dims_hbm,
    out, left_out, right_out,
    psi, left, right, conn, qrow, qclass, dims, right_rows, code, wide, sems,
):
    sec, width = psi.shape[0], psi.shape[1]
    terms, classes = left.shape[0], left.shape[1]
    half, nsec = width // 2, conn.shape[1]
    pairs = (
        (right_hbm, right), (conn_hbm, conn), (left_hbm, left),
        (qclass_hbm, qclass), (qclass_hbm, qrow), (dims_hbm, dims), (psi_hbm, psi),
    )
    copies = [pltpu.make_async_copy(a, b, sems.at[i]) for i, (a, b) in enumerate(pairs)]
    for copy in copies:
        copy.start()
    order = split_order(width)
    edge = jnp.maximum(iota((width, width), 0), iota((width, width), 1))
    first = lax.axis_index("blk") * sec
    code[...] = jnp.zeros_like(code)
    copies[0].wait()
    for t in range(terms):
        for q in range(classes):
            right_rows[t, q] = matmul(order, right[t, q])
            right_out[t, q] = matmul_nt(right[t, q], order).astype(BF16)
    copies[1].wait()
    for t in range(terms):
        high = conn[t : t + 1, :] // CODE_BASE
        low = conn[t : t + 1, :] - high * CODE_BASE
        for j in range(nsec // width):
            code[pl.ds(j, 1), :] = high[:, j * width : (j + 1) * width].astype(F32)
            code[pl.ds(nsec // width + j, 1), :] = low[:, j * width : (j + 1) * width].astype(F32)
        left_out[t, classes * width :, :] = code[...].astype(BF16)
    copies[2].wait()
    for t in range(terms):
        for q in range(classes):
            left_out[t, q * width : (q + 1) * width, :] = matmul(order, left[t, q]).astype(BF16)
    for copy in copies[3:]:
        copy.wait()
    for c in range(sec):
        own = first + c
        masked = jnp.where(edge < dims[0, own], psi[c].astype(F32), 0.0).astype(BF16)
        target = jnp.sum(jnp.where(conn[...] == own, qrow[...].astype(F32), 0.0), axis=1, keepdims=True)
        for t in range(terms):
            contracted = matmul(left[t, qclass[0, own]], masked).astype(BF16)
            chosen = right_rows[t, 0]
            for q in range(1, classes):
                chosen = jnp.where(target[t : t + 1, :] == float(q), right_rows[t, q], chosen)
            image = matmul_nt(chosen.astype(BF16), contracted)
            pair = t * sec + c
            for j in range(wide.shape[0]):
                r, at = j // (width // LANES), j % (width // LANES) * LANES
                wide[j, pl.ds(pair, half, stride=terms * sec), :] = image[
                    r * half : (r + 1) * half, at : at + LANES
                ]
    for j in range(wide.shape[0]):
        out[:, j * LANES : (j + 1) * LANES] = wide[j].astype(BF16)


def gather_copies(sources, into, sems):
    each = into.shape[0] // len(sources)
    copies = [
        pltpu.make_async_copy(a, into.at[pl.ds(i * each, each)], sems.at[i])
        for i, a in enumerate(sources)
    ]
    for copy in copies:
        copy.start()
    return copies


def middle_kernel(classes, parts, qcol, *rest):
    sources, (out, left, wide, sems) = rest[:-4], rest[-4:]
    terms, nsec, width = left.shape[0], parts.shape[1], left.shape[2]
    half = width // 2
    copies = gather_copies(sources, left, sems)
    total = parts[0].astype(F32)
    for x in range(1, parts.shape[0]):
        total = total + parts[x].astype(F32)
    for j in range(total.shape[1] // LANES):
        wide[4, pl.ds(j, nsec, stride=terms), :] = total[:, j * LANES : (j + 1) * LANES]
    for j in range(total.shape[1] // LANES, terms):
        wide[4, pl.ds(j, nsec, stride=terms), :] = jnp.zeros((nsec, LANES), F32)
    chosen = []
    for q in range(classes):
        kept = jnp.where(qcol[...] == q, total, 0.0).astype(BF16)
        chosen.append(jnp.concatenate([kept[:, :width], kept[:, width:]], axis=0))
    for t in range(terms):
        if t % (terms // len(copies)) == 0:
            copies[t // (terms // len(copies))].wait()
        image = matmul_nt(left[t, 0:width, :], chosen[0])
        for q in range(1, classes):
            image = image + matmul_nt(left[t, q * width : (q + 1) * width, :], chosen[q])
        for j in range(4):
            ri, r = j // 2, j % 2
            wide[j, pl.ds(t, half, stride=terms), :] = image[
                ri * half : (ri + 1) * half, r * nsec : (r + 1) * nsec
            ]
    for j in range(5):
        out[:, j * LANES : (j + 1) * LANES] = wide[j].astype(BF16)


def target_kernel(spread, moved, conn, qrow, dims, *rest):
    sources, (out, right, wide, images, route, sector, sems) = rest[:-7], rest[-7:]
    terms, classes, width = right.shape[0], right.shape[1], right.shape[2]
    half, nsec = width // 2, conn.shape[1]
    blk, x = lax.axis_index("blk"), lax.axis_index("term")
    copies = gather_copies(sources, right, sems)
    for j in range(5):
        wide[j] = moved[:, j * LANES : (j + 1) * LANES].astype(F32)
    for ih in range(2):
        for r in range(2):
            sector[ih, pl.ds(r, half, stride=2), :] = wide[4, pl.ds(2 * r + ih, half, stride=terms), :]
    source = iota((LANES, nsec), 0) * spread + x
    for t in range(terms):
        route[t * LANES : (t + 1) * LANES, :] = (conn[t : t + 1, :] == source).astype(F32).astype(BF16)
    classes_row = jnp.broadcast_to(qrow[...].astype(F32), (8, nsec)).astype(BF16)
    target = matmul_nt(classes_row, route[...])
    for t in range(terms):
        if t % (terms // len(copies)) == 0:
            copies[t // (terms // len(copies))].wait()
        both = jnp.concatenate(
            [
                jnp.concatenate(
                    [wide[2 * ri + r, pl.ds(t, half, stride=terms), :] for r in range(2)], axis=0
                )
                for ri in range(2)
            ],
            axis=1,
        ).astype(BF16)
        pick = target[0:1, t * LANES : (t + 1) * LANES]
        pick = jnp.concatenate([pick, pick], axis=1)
        image = matmul(right[t, 0], both)
        for q in range(1, classes):
            image = jnp.where(pick == float(q), matmul(right[t, q], both), image)
        high = image.astype(BF16)
        low = (image - high.astype(F32)).astype(BF16)
        for ri in range(2):
            at = slice(t * LANES, (t + 1) * LANES)
            images[0, ri * width : (ri + 1) * width, at] = high[:, ri * LANES : (ri + 1) * LANES]
            images[1, ri * width : (ri + 1) * width, at] = low[:, ri * LANES : (ri + 1) * LANES]
    total = matmul(images[0], route[...]) + matmul(images[1], route[...])
    line = iota((2 * width, 1), 0)
    ri = (line >= width).astype(jnp.int32)
    edge = jnp.maximum(2 * blk + ri, line - ri * width)
    total = jnp.where(edge < dims[...], total, 0.0).astype(BF16)
    turned = [sector[ih].T.astype(BF16) for ih in range(2)]
    each = nsec // out.shape[0]
    for to in range(out.shape[0]):
        out[to, : 2 * width, :] = total[:, to * each : (to + 1) * each]
        for lh in range(2):
            for ih in range(2):
                first = 2 * width + lh * width + ih * LANES
                out[to, first : first + LANES, :] = turned[ih][:, lh * LANES : (lh + 1) * LANES]


def last_kernel(parts, one, two):
    width = one.shape[1]
    total = parts[0, : 2 * width, :].astype(F32)
    for x in range(1, parts.shape[0]):
        total = total + parts[x, : 2 * width, :].astype(F32)
    two[...] = total.T.astype(BF16)
    for x in range(parts.shape[0]):
        for lh in range(2):
            one[x, :, lh * LANES : (lh + 1) * LANES] = parts[
                x, (2 + lh) * width : (3 + lh) * width, :
            ]


def call(kernel, out_shape, in_specs, scratch, vmem_bytes, flops, *operands):
    vmem = pl.BlockSpec(memory_space=pltpu.VMEM)
    return pl.pallas_call(
        kernel,
        out_shape=out_shape,
        in_specs=in_specs,
        out_specs=jax.tree.map(lambda _: vmem, out_shape),
        scratch_shapes=scratch,
        compiler_params=pltpu.CompilerParams(vmem_limit_bytes=vmem_bytes),
        cost_estimate=pl.CostEstimate(flops=flops, bytes_accessed=6 << 20, transcendentals=0),
    )(*operands)


def from_all(a, axis):
    n = lax.axis_size(axis)
    return [a] + [lax.ppermute(a, axis, [(i, (i + d) % n) for i in range(n)]) for d in range(1, n)]


def on_device(psi, left_env, right_env, connect, qclass, sector_dims):
    nblk = lax.axis_size("blk")
    nterm = lax.axis_size("term")
    sec, width = psi.shape[0], psi.shape[1]
    band = width // nblk
    nsec = qclass.shape[0]
    terms, classes = left_env.shape[0], left_env.shape[1]
    pairs = terms * sec
    kept = nsec // nterm
    all_terms = terms * nterm
    blk = lax.axis_index("blk")
    x = lax.axis_index("term")
    vmem = pl.BlockSpec(memory_space=pltpu.VMEM)
    hbm = pl.BlockSpec(memory_space=pl.ANY)
    bf16 = lambda *shape: jax.ShapeDtypeStruct(shape, BF16)
    q_row, d_row = qclass[None, :], sector_dims[None, :]

    def by_owner(a):
        return a.reshape(nblk, sec).T.reshape(nsec)

    sent, left_mine, right_mine = call(
        source_kernel,
        (
            bf16(nblk * pairs, band * width),
            bf16(terms, classes * width + CODE_ROWS, width),
            bf16(terms, classes, width, width),
        ),
        [hbm] * 6,
        [
            pltpu.VMEM(psi.shape, BF16),
            pltpu.VMEM(left_env.shape, BF16),
            pltpu.VMEM(right_env.shape, BF16),
            pltpu.VMEM(connect.shape, jnp.int32),
            pltpu.VMEM(q_row.shape, jnp.int32),
            pltpu.SMEM(q_row.shape, jnp.int32),
            pltpu.SMEM(d_row.shape, jnp.int32),
            pltpu.VMEM(right_env.shape, F32),
            pltpu.VMEM((CODE_ROWS, width), F32),
            pltpu.VMEM((band * width // LANES, nblk * pairs, LANES), F32),
            pltpu.SemaphoreType.DMA((7,)),
        ],
        None,
        (2 * pairs + 3 * terms * classes) * 2 * width**3,
        psi, left_env, right_env, connect, q_row, d_row,
    )
    lefts = from_all(left_mine, "term")
    rights = from_all(right_mine, "term")
    code = jnp.concatenate([a[:, classes * width :, :] for a in lefts], axis=0).astype(F32)
    halves = nsec // width
    conn_all = CODE_BASE * code[:, :halves].reshape(all_terms, nsec) + code[
        :, halves : 2 * halves
    ].reshape(all_terms, nsec)
    conn_all = conn_all.astype(jnp.int32)

    k = jnp.arange(nblk * pairs, dtype=jnp.int32)
    k_term = (k // sec) % terms
    k_sector = (k // pairs) * sec + k % sec
    wanted = jnp.zeros((nsec, k.shape[0]), jnp.int32)
    for t in range(terms):
        wanted = jnp.where(k_term[None, :] == t, by_owner(connect[t])[:, None], wanted)
    route = (wanted == k_sector[None, :]).astype(BF16)
    element = jnp.arange(band * width, dtype=jnp.int32)
    edge = jnp.maximum(blk * band + element // width, element % width)
    keep = edge[None, :] < by_owner(sector_dims)[:, None]
    qcol = lax.dynamic_slice_in_dim(by_owner(qclass), x * kept, kept)[:, None]

    moved = lax.all_to_all(
        sent.reshape(nblk, pairs, band * width), "blk", split_axis=0, concat_axis=0, tiled=True
    ).reshape(nblk * pairs, band * width)
    total = jnp.where(keep, matmul(route, moved), 0.0).astype(BF16)
    parts = lax.all_to_all(
        total.reshape(nterm, kept, band * width), "term", split_axis=0, concat_axis=0, tiled=True
    )
    sent = call(
        functools.partial(middle_kernel, classes),
        bf16(nblk * all_terms, band * width + LANES),
        [vmem, vmem] + [hbm] * nterm,
        [
            pltpu.VMEM((all_terms,) + left_mine.shape[1:], BF16),
            pltpu.VMEM((5, nblk * all_terms, LANES), F32),
            pltpu.SemaphoreType.DMA((nterm,)),
        ],
        20 << 20,
        2 * all_terms * classes * width**3,
        parts, qcol, *lefts,
    )
    moved = lax.all_to_all(
        sent.reshape(nblk, all_terms, -1), "blk", split_axis=0, concat_axis=0, tiled=True
    ).reshape(nblk * all_terms, -1)
    sent = call(
        functools.partial(target_kernel, sec),
        bf16(nterm, 4 * width, kept),
        [vmem, vmem, vmem, vmem] + [hbm] * nterm,
        [
            pltpu.VMEM((all_terms,) + right_mine.shape[1:], BF16),
            pltpu.VMEM((5, nblk * all_terms, LANES), F32),
            pltpu.VMEM((2, band * width, all_terms * LANES), BF16),
            pltpu.VMEM((all_terms * LANES, nsec), BF16),
            pltpu.VMEM((2, width, LANES), F32),
            pltpu.SemaphoreType.DMA((nterm,)),
        ],
        28 << 20,
        2 * all_terms * (classes * width**3 + 2 * 2 * width * LANES * nsec),
        moved, conn_all, q_row, d_row, *rights,
    )
    parts = lax.all_to_all(sent, "term", split_axis=0, concat_axis=0, tiled=True)
    sigma_one, two = call(
        last_kernel,
        (bf16(sec, width, width), bf16(kept, band * width)),
        [vmem],
        [],
        16 << 20,
        0,
        parts,
    )
    return (sigma_one, two.reshape(kept, band, width))


def solution(mesh):
    placed = (
        P("blk", None, None),
        P("term", None, None, None),
        P("term", None, None, None),
        P("term", None),
        P(),
        P(),
    )
    return jax.shard_map(
        on_device,
        mesh=mesh,
        in_specs=placed,
        out_specs=(P("blk", None, None), P("term", "blk", None)),
        check_vma=False,
    )
```

time: 290 us -> 199 us (0.69)
  blocking collectives: 135 us -> 18.4 us
  waiting for transfers between devices: 76.4 us -> 108 us
  starting transfers between devices: 19.3 us -> 50.3 us
  local copies, waits for them, and re-layouts: 24.5 us -> 8.18 us
  between operations: 14.4 us -> 0.92 us
  other arithmetic: 11.7 us -> 0.06 us
  Pallas kernels: 0 us -> 11.5 us
  matrix products: 7.24 us -> 1.57 us
    all_to_all x2 -> x1, blocking collectives: 102 us -> 18.4 us  [on_device(): lax.all_to_all(sent, 'term', split_axis=0, concat_axis=0, tiled=True)]
    psum x1 -> x0, blocking collectives: 33.4 us -> none  [on_device(): summed = lax.psum(first_total, 'term').astype(jnp.bfloat16)]
    all_to_all x1 -> x3, waiting for transfers between devices: 55 us -> 87.1 us  [the longest x1 43.4 us: on_device(): lax.all_to_all(sent.reshape(nblk, pairs, band * width), 'blk', split_axis...]
    reduce_scatter x1 -> x0, waiting for transfers between devices: 21.3 us -> none  [on_device(): lax.psum_scatter(second_total, 'term', scatter_dimension=0, tiled=True)]
    ppermute x0 -> x6, waiting for transfers between devices: none -> 20.4 us  [from_all(): lax.ppermute(a, axis, [(i, (i + d) % n) for i in range(n)])]
    ppermute x0 -> x6, starting transfers between devices: none -> 20.4 us  [from_all(): lax.ppermute(a, axis, [(i, (i + d) % n) for i in range(n)])]
    gather x5 -> x0, local copies, waits for them, and re-layouts: 13.3 us -> none  [the longest x4 12.7 us: partial_terms(): jnp.take(moved[which], connect[which], axis=0).reshape(nsec * band, width)]
    pallas_call x0 -> x4, Pallas kernels: none -> 11.5 us  [call(): pl.pallas_call(kernel, out_shape=out_shape, in_specs=in_specs, out_specs=...]
  transfers between devices with their start and end apart: 2 -> 9, of which waited for: 2 -> 5; matrix products, arithmetic and copies ran while one was open for 0% -> 1% of each run, Pallas kernels for 0% -> 0%
where the time goes in v2:
time: 199 us
  waiting for transfers between devices  108 us (54%)
  starting transfers between devices  50.3 us (25%)
  blocking collectives  18.4 us (9%)
  Pallas kernels  11.5 us (6%)
  local copies, waits for them, and re-layouts  8.18 us (4%)
    all_to_all x1, waiting for transfers between devices, on_device(): lax.all_to_all(sent.reshape(nblk, pairs, band * width), 'blk', split_axis...  43.4 us
    all_to_all x1, waiting for transfers between devices, on_device(): lax.all_to_all(sent.reshape(nblk, all_terms, -1), 'blk', split_axis=0, co...  34.2 us
    ppermute x6, waiting for transfers between devices, from_all(): lax.ppermute(a, axis, [(i, (i + d) % n) for i in range(n)])  20.4 us
    ppermute x6, starting transfers between devices, from_all(): lax.ppermute(a, axis, [(i, (i + d) % n) for i in range(n)])  20.4 us
    all_to_all x1, starting transfers between devices, on_device(): lax.all_to_all(sent.reshape(nblk, pairs, band * width), 'blk', split_axis...  19.3 us
    all_to_all x1, blocking collectives, on_device(): lax.all_to_all(sent, 'term', split_axis=0, concat_axis=0, tiled=True)  18.4 us
    pallas_call x4, Pallas kernels, call(): pl.pallas_call(kernel, out_shape=out_shape, in_specs=in_specs, out_specs=...  11.5 us
    all_to_all x1, waiting for transfers between devices, on_device(): lax.all_to_all(total.reshape(nterm, kept, band * width), 'term', split_ax...  9.54 us
  transfers between devices with their start and end apart: 9, of which 5 were waited for; matrix products, arithmetic and copies ran while one was open for 1% of the time, Pallas kernels for 0%

profile of v2, /device:TPU:32, one launch (start us, length us, event | category | flops | bytes accessed | tf_op | source)
XLA Modules:
  0.0 198.5 jit_solution(5878021510731537061)
XLA Ops:
  0.6 4.0 %shard_map.77 = (bf16[1024,512]{1,0:T(8,128)(2,1)}, bf16[2,528,256]{2,1,0:T(8,128)(2,1)}, bf16[2,2,256,256]{3,2,1,0:T(8,128)(2,1)}) custom-call(bf16[4,256,256]{2,1,0:T(8,128)(2,1)} %psi_hbm.1, bf16[2,2,256,256]{3,2,1,0:T(8,128)(2,1)} %left_hbm.1, bf16[2,2,256,256]{3,2,1,0:T(8,128)(2,1)} %right_hbm.1, s32[2,512]{1,0:T(2,128)} %conn_hbm.1, ...), custom_call_target="tpu_custom_call" | custom-call | flops 939524096 | bytes 6291456 | tf_op jit(solution)/shard_map/pallas_call | solution.py:205
  4.7 19.3 %all-to-all-start = ((bf16[128,8,512]{2,1,0:T(8,128)(2,1)}), bf16[128,8,512]{2,1,0:T(8,128)(2,1)S(1)}, u32[]{:S(2)}, u32[]{:S(2)}) async-start(bf16[128,8,512]{2,1,0:T(8,128)(2,1)} %bitcast.28), calls=%async_computation | async-start | bytes 2097152 | tf_op jit(solution)/shard_map/all_to_all | solution.py:287
  24.0 3.4 %collective-permute-start = (bf16[2,528,256]{2,1,0:T(8,128)(2,1)S(1)}, bf16[2,528,256]{2,1,0:T(8,128)(2,1)S(1)}, u32[]{:S(2)}, u32[]{:S(2)}) collective-permute-start(bf16[2,528,256]{2,1,0:T(8,128)(2,1)S(1)} %copy-done), channel_id=1, source_target_pairs={{0,1},{1,2},{2,3},{3,0},{4,5},{5,6},{6,7},{7,4},{8,9},{9,10},{10,1... | collective-permute-start | bytes 1622024 | tf_op jit(solution)/shard_map/ppermute | solution.py:218
  27.4 4.6 %collective-permute-start.1 = (bf16[2,528,256]{2,1,0:T(8,128)(2,1)S(1)}, bf16[2,528,256]{2,1,0:T(8,128)(2,1)S(1)}, u32[]{:S(2)}, u32[]{:S(2)}) collective-permute-start(bf16[2,528,256]{2,1,0:T(8,128)(2,1)S(1)} %copy-done), channel_id=1, source_target_pairs={{0,2},{1,3},{2,0},{3,1},{4,6},{5,7},{6,4},{7,5},{8,10},{9,11},{10,... | collective-permute-start | bytes 1622024 | tf_op jit(solution)/shard_map/ppermute | solution.py:218
  32.1 3.3 %collective-permute-start.2 = (bf16[2,528,256]{2,1,0:T(8,128)(2,1)S(1)}, bf16[2,528,256]{2,1,0:T(8,128)(2,1)S(1)}, u32[]{:S(2)}, u32[]{:S(2)}) collective-permute-start(bf16[2,528,256]{2,1,0:T(8,128)(2,1)S(1)} %copy-done), channel_id=1, source_target_pairs={{0,3},{1,0},{2,1},{3,2},{4,7},{5,4},{6,5},{7,6},{8,11},{9,8},{10,9... | collective-permute-start | bytes 1622024 | tf_op jit(solution)/shard_map/ppermute | solution.py:218
  35.4 0.1 reshape.112
  35.6 0.1 reshape_squeeze.6
  35.8 0.1 reshape_squeeze.7
  36.1 43.4 %all-to-all-done = bf16[128,8,512]{2,1,0:T(8,128)(2,1)S(1)} async-done(((bf16[128,8,512]{2,1,0:T(8,128)(2,1)}), bf16[128,8,512]{2,1,0:T(8,128)(2,1)S(1)}, u32[]{:S(2)}, u32[]{:S(2)}) %all-to-all-start) | async-done | bytes 1048608 | tf_op jit(solution)/shard_map/all_to_all | solution.py:287
  79.5 1.6 fusion.2
  81.0 4.3 %all-to-all-start.1 = ((bf16[4,128,512]{2,1,0:T(8,128)(2,1)}), bf16[4,128,512]{2,1,0:T(8,128)(2,1)S(1)}, u32[]{:S(2)}, u32[]{:S(2)}) async-start(bf16[4,128,512]{2,1,0:T(8,128)(2,1)} %bitcast.29), calls=%async_computation.1 | async-start | bytes 1048576 | tf_op jit(solution)/shard_map/all_to_all | solution.py:291
  85.6 0.1 copy.13.qcol
  85.7 9.5 %all-to-all-done.1.parts = bf16[4,128,512]{2,1,0:T(8,128)(2,1)S(1)} async-done(((bf16[4,128,512]{2,1,0:T(8,128)(2,1)}), bf16[4,128,512]{2,1,0:T(8,128)(2,1)S(1)}, u32[]{:S(2)}, u32[]{:S(2)}) %all-to-all-start.1) | async-done | bytes 524320 | tf_op jit(solution)/shard_map/all_to_all | solution.py:291
  95.3 3.1 %shard_map.78 = bf16[1024,640]{1,0:T(8,128)(2,1)} custom-call(bf16[4,128,512]{2,1,0:T(8,128)(2,1)S(1)} %all-to-all-done.1.parts, s32[128,1]{1,0:T(8,128)S(1)} %copy.13.qcol, bf16[2,528,256]{2,1,0:T(8,128)(2,1)S(1)} %copy-done, bf16[2,528,256]{2,1,0:T(8,128)(2,1)S(1)} %collective-permute-done.rest_1_, ...), custom_call_target="tpu_custom_call" | custom-call | flops 536870912 | bytes 6291456 | tf_op jit(solution)/shard_map/pallas_call | solution.py:205
  98.4 6.4 %all-to-all-start.2 = ((bf16[128,8,640]{2,1,0:T(8,128)(2,1)}), bf16[128,8,640]{2,1,0:T(8,128)(2,1)S(1)}, u32[]{:S(2)}, u32[]{:S(2)}) async-start(bf16[128,8,640]{2,1,0:T(8,128)(2,1)} %bitcast.14), calls=%async_computation.2 | async-start | bytes 2621440 | tf_op jit(solution)/shard_map/all_to_all | solution.py:307
  104.8 2.5 %collective-permute-start.3 = (bf16[2,2,256,256]{3,2,1,0:T(8,128)(2,1)}, bf16[2,2,256,256]{3,2,1,0:T(8,128)(2,1)S(1)}, u32[]{:S(2)}, u32[]{:S(2)}) collective-permute-start(bf16[2,2,256,256]{3,2,1,0:T(8,128)(2,1)} %get-tuple-element.9.rest_0_), channel_id=1, source_target_pairs={{0,1},{1,2},{2,3},{3,0},{4,5},{5,6},{6,7},{7,4},{8,9},{9,10},{10,1... | collective-permute-start | bytes 1572872 | tf_op jit(solution)/shard_map/ppermute | solution.py:218
  107.3 4.0 %collective-permute-start.4 = (bf16[2,2,256,256]{3,2,1,0:T(8,128)(2,1)}, bf16[2,2,256,256]{3,2,1,0:T(8,128)(2,1)S(1)}, u32[]{:S(2)}, u32[]{:S(2)}) collective-permute-start(bf16[2,2,256,256]{3,2,1,0:T(8,128)(2,1)} %get-tuple-element.9.rest_0_), channel_id=1, source_target_pairs={{0,2},{1,3},{2,0},{3,1},{4,6},{5,7},{6,4},{7,5},{8,10},{9,11},{10,... | collective-permute-start | bytes 1572872 | tf_op jit(solution)/shard_map/ppermute | solution.py:218
  111.3 2.5 %collective-permute-start.5 = (bf16[2,2,256,256]{3,2,1,0:T(8,128)(2,1)}, bf16[2,2,256,256]{3,2,1,0:T(8,128)(2,1)S(1)}, u32[]{:S(2)}, u32[]{:S(2)}) collective-permute-start(bf16[2,2,256,256]{3,2,1,0:T(8,128)(2,1)} %get-tuple-element.9.rest_0_), channel_id=1, source_target_pairs={{0,3},{1,0},{2,1},{3,2},{4,7},{5,4},{6,5},{7,6},{8,11},{9,8},{10,9... | collective-permute-start | bytes 1572872 | tf_op jit(solution)/shard_map/ppermute | solution.py:218
  113.9 19.4 %collective-permute-done.3.rest_1_ = bf16[2,2,256,256]{3,2,1,0:T(8,128)(2,1)S(1)} collective-permute-done((bf16[2,2,256,256]{3,2,1,0:T(8,128)(2,1)}, bf16[2,2,256,256]{3,2,1,0:T(8,128)(2,1)S(1)}, u32[]{:S(2)}, u32[]{:S(2)}) %collective-permute-start.3) | collective-permute-done | bytes 524320 | tf_op jit(solution)/shard_map/ppermute | solution.py:218
  133.3 0.8 copy-done.4
  134.1 0.8 copy-done.6
  134.9 1.0 collective-permute-done.5.rest_3_
  135.9 0.8 copy-done.8
  136.7 34.2 %all-to-all-done.2 = bf16[128,8,640]{2,1,0:T(8,128)(2,1)S(1)} async-done(((bf16[128,8,640]{2,1,0:T(8,128)(2,1)}), bf16[128,8,640]{2,1,0:T(8,128)(2,1)S(1)}, u32[]{:S(2)}, u32[]{:S(2)}) %all-to-all-start.2) | async-done | bytes 1310752 | tf_op jit(solution)/shard_map/all_to_all | solution.py:307
  170.9 1.0 copy-done.3
  171.9 1.0 copy-done.5
  173.0 1.0 copy-done.7
  174.0 1.0 copy-done.9
  175.1 3.4 %shard_map.79 = bf16[4,1024,128]{2,1,0:T(8,128)(2,1)S(1)} custom-call(bf16[1024,640]{1,0:T(8,128)(2,1)S(1)} %bitcast.22, s32[8,512]{1,0:T(8,128)S(1)} %bitcast.23, s32[1,512]{1,0:T(1,128)S(1)} %bitcast.25, s32[1,512]{1,0:T(1,128)S(1)} %bitcast.27, bf16[2,2,256,256]{3,2,1,0:T(8,128)(2,1)S(1)} %copy-done.3, bf16[2,2,256,256]{3,2,1,0:T(8,128)(2,1)S(1)} %copy-done.5, ...), custom_call_target="tpu_custom_call" | custom-call | flops 1610612736 | bytes 6291456 | tf_op jit(solution)/shard_map/pallas_call | solution.py:205
  178.5 18.4 %all_to_all.20.parts = bf16[4,1024,128]{2,1,0:T(8,128)(2,1)S(1)} all-to-all(bf16[4,1024,128]{2,1,0:T(8,128)(2,1)S(1)} %shard_map.79), channel_id=1, replica_groups=mesh['blk'=128,'term'=4] {'term'}, dimensions={0} | all-to-all | bytes 2097152 | tf_op jit(solution)/shard_map/all_to_all | solution.py:326
  196.9 0.9 shard_map.80
  197.8 0.7 reshape.120
  (35 shorter events, 0.6 us)
Async XLA Ops:
  4.7 19.4 %copy-start = (bf16[2,528,256]{2,1,0:T(8,128)(2,1)S(1)}, bf16[2,528,256]{2,1,0:T(8,128)(2,1)}, u32[]{:S(2)}) copy-start(bf16[2,528,256]{2,1,0:T(8,128)(2,1)} %get-tuple-element.8.rest_0_) | copy-start | bytes 1622020
  4.7 30.8 %copy-start.2 = (s32[512]{0:T(512)S(1)}, s32[512]{0:T(512)}, u32[]{:S(2)}) copy-start(s32[512]{0:T(512)} %param.11) | copy-start | bytes 6148
  4.7 30.9 %copy-start.10 = (s32[2,512]{1,0:T(2,128)S(1)}, s32[2,512]{1,0:T(2,128)}, u32[]{:S(2)}) copy-start(s32[2,512]{1,0:T(2,128)} %conn_hbm.1) | copy-start | bytes 12292
  4.7 74.8 %all-to-all-start = ((bf16[128,8,512]{2,1,0:T(8,128)(2,1)}), bf16[128,8,512]{2,1,0:T(8,128)(2,1)S(1)}, u32[]{:S(2)}, u32[]{:S(2)}) async-start(bf16[128,8,512]{2,1,0:T(8,128)(2,1)} %bitcast.28), calls=%async_computation | async-start | bytes 2097152 | tf_op jit(solution)/shard_map/all_to_all | solution.py:287
  24.0 61.7 %collective-permute-start = (bf16[2,528,256]{2,1,0:T(8,128)(2,1)S(1)}, bf16[2,528,256]{2,1,0:T(8,128)(2,1)S(1)}, u32[]{:S(2)}, u32[]{:S(2)}) collective-permute-start(bf16[2,528,256]{2,1,0:T(8,128)(2,1)S(1)} %copy-done), channel_id=1, source_target_pairs={{0,1},{1,2},{2,3},{3,0},{4,5},{5,6},{6,7},{7,4},{8,9},{9,10},{10,1... | collective-permute-start | bytes 1622024 | tf_op jit(solution)/shard_map/ppermute | solution.py:218
  27.4 58.3 %collective-permute-start.1 = (bf16[2,528,256]{2,1,0:T(8,128)(2,1)S(1)}, bf16[2,528,256]{2,1,0:T(8,128)(2,1)S(1)}, u32[]{:S(2)}, u32[]{:S(2)}) collective-permute-start(bf16[2,528,256]{2,1,0:T(8,128)(2,1)S(1)} %copy-done), channel_id=1, source_target_pairs={{0,2},{1,3},{2,0},{3,1},{4,6},{5,7},{6,4},{7,5},{8,10},{9,11},{10,... | collective-permute-start | bytes 1622024 | tf_op jit(solution)/shard_map/ppermute | solution.py:218
  32.1 53.7 %collective-permute-start.2 = (bf16[2,528,256]{2,1,0:T(8,128)(2,1)S(1)}, bf16[2,528,256]{2,1,0:T(8,128)(2,1)S(1)}, u32[]{:S(2)}, u32[]{:S(2)}) collective-permute-start(bf16[2,528,256]{2,1,0:T(8,128)(2,1)S(1)} %copy-done), channel_id=1, source_target_pairs={{0,3},{1,0},{2,1},{3,2},{4,7},{5,4},{6,5},{7,6},{8,11},{9,8},{10,9... | collective-permute-start | bytes 1622024 | tf_op jit(solution)/shard_map/ppermute | solution.py:218
  79.5 5.9 %copy-start.1 = (s32[512]{0:T(512)S(1)}, s32[512]{0:T(512)}, u32[]{:S(2)}) copy-start(s32[512]{0:T(512)} %param.10) | copy-start | bytes 6148
  81.0 14.2 %all-to-all-start.1 = ((bf16[4,128,512]{2,1,0:T(8,128)(2,1)}), bf16[4,128,512]{2,1,0:T(8,128)(2,1)S(1)}, u32[]{:S(2)}, u32[]{:S(2)}) async-start(bf16[4,128,512]{2,1,0:T(8,128)(2,1)} %bitcast.29), calls=%async_computation.1 | async-start | bytes 1048576 | tf_op jit(solution)/shard_map/all_to_all | solution.py:291
  98.4 72.5 %all-to-all-start.2 = ((bf16[128,8,640]{2,1,0:T(8,128)(2,1)}), bf16[128,8,640]{2,1,0:T(8,128)(2,1)S(1)}, u32[]{:S(2)}, u32[]{:S(2)}) async-start(bf16[128,8,640]{2,1,0:T(8,128)(2,1)} %bitcast.14), calls=%async_computation.2 | async-start | bytes 2621440 | tf_op jit(solution)/shard_map/all_to_all | solution.py:307
  104.8 28.5 %collective-permute-start.3 = (bf16[2,2,256,256]{3,2,1,0:T(8,128)(2,1)}, bf16[2,2,256,256]{3,2,1,0:T(8,128)(2,1)S(1)}, u32[]{:S(2)}, u32[]{:S(2)}) collective-permute-start(bf16[2,2,256,256]{3,2,1,0:T(8,128)(2,1)} %get-tuple-element.9.rest_0_), channel_id=1, source_target_pairs={{0,1},{1,2},{2,3},{3,0},{4,5},{5,6},{6,7},{7,4},{8,9},{9,10},{10,1... | collective-permute-start | bytes 1572872 | tf_op jit(solution)/shard_map/ppermute | solution.py:218
  107.3 26.8 %collective-permute-start.4 = (bf16[2,2,256,256]{3,2,1,0:T(8,128)(2,1)}, bf16[2,2,256,256]{3,2,1,0:T(8,128)(2,1)S(1)}, u32[]{:S(2)}, u32[]{:S(2)}) collective-permute-start(bf16[2,2,256,256]{3,2,1,0:T(8,128)(2,1)} %get-tuple-element.9.rest_0_), channel_id=1, source_target_pairs={{0,2},{1,3},{2,0},{3,1},{4,6},{5,7},{6,4},{7,5},{8,10},{9,11},{10,... | collective-permute-start | bytes 1572872 | tf_op jit(solution)/shard_map/ppermute | solution.py:218
  111.3 24.6 %collective-permute-start.5 = (bf16[2,2,256,256]{3,2,1,0:T(8,128)(2,1)}, bf16[2,2,256,256]{3,2,1,0:T(8,128)(2,1)S(1)}, u32[]{:S(2)}, u32[]{:S(2)}) collective-permute-start(bf16[2,2,256,256]{3,2,1,0:T(8,128)(2,1)} %get-tuple-element.9.rest_0_), channel_id=1, source_target_pairs={{0,3},{1,0},{2,1},{3,2},{4,7},{5,4},{6,5},{7,6},{8,11},{9,8},{10,9... | collective-permute-start | bytes 1572872 | tf_op jit(solution)/shard_map/ppermute | solution.py:218
  133.3 0.8 copy-start.4
  134.1 0.8 copy-start.6
  135.9 0.8 copy-start.8
  170.9 1.0 copy-start.3
  171.9 1.0 copy-start.5
  173.0 1.0 copy-start.7
  174.0 1.0 copy-start.9

commit v3 on v2

--- a/solution.py
+++ b/solution.py
@@ -35,12 +35,12 @@
 
 def source_kernel(
     psi_hbm, left_hbm, right_hbm, conn_hbm, qclass_hbm, dims_hbm,
-    out, left_out, right_out,
-    psi, left, right, conn, qrow, qclass, dims, right_rows, code, wide, sems,
+    out,
+    psi, left, right, conn, qrow, qclass, dims, right_rows, wide, sems,
 ):
     sec, width = psi.shape[0], psi.shape[1]
     terms, classes = left.shape[0], left.shape[1]
-    half, nsec = width // 2, conn.shape[1]
+    half = width // 2
     pairs = (
         (right_hbm, right), (conn_hbm, conn), (left_hbm, left),
         (qclass_hbm, qclass), (qclass_hbm, qrow), (dims_hbm, dims), (psi_hbm, psi),
@@ -51,25 +51,11 @@
     order = split_order(width)
     edge = jnp.maximum(iota((width, width), 0), iota((width, width), 1))
     first = lax.axis_index("blk") * sec
-    code[...] = jnp.zeros_like(code)
     copies[0].wait()
     for t in range(terms):
         for q in range(classes):
             right_rows[t, q] = matmul(order, right[t, q])
-            right_out[t, q] = matmul_nt(right[t, q], order).astype(BF16)
-    copies[1].wait()
-    for t in range(terms):
-        high = conn[t : t + 1, :] // CODE_BASE
-        low = conn[t : t + 1, :] - high * CODE_BASE
-        for j in range(nsec // width):
-            code[pl.ds(j, 1), :] = high[:, j * width : (j + 1) * width].astype(F32)
-            code[pl.ds(nsec // width + j, 1), :] = low[:, j * width : (j + 1) * width].astype(F32)
-        left_out[t, classes * width :, :] = code[...].astype(BF16)
-    copies[2].wait()
-    for t in range(terms):
-        for q in range(classes):
-            left_out[t, q * width : (q + 1) * width, :] = matmul(order, left[t, q]).astype(BF16)
-    for copy in copies[3:]:
+    for copy in copies[1:]:
         copy.wait()
     for c in range(sec):
         own = first + c
@@ -91,22 +77,28 @@
         out[:, j * LANES : (j + 1) * LANES] = wide[j].astype(BF16)
 
 
-def gather_copies(sources, into, sems):
-    each = into.shape[0] // len(sources)
-    copies = [
-        pltpu.make_async_copy(a, into.at[pl.ds(i * each, each)], sems.at[i])
-        for i, a in enumerate(sources)
-    ]
-    for copy in copies:
-        copy.start()
-    return copies
+def order_kernel(left, right, conn, left_out, right_out, code):
+    terms, classes, width = left.shape[0], left.shape[1], left.shape[2]
+    nsec = conn.shape[1]
+    order = split_order(width)
+    code[...] = jnp.zeros_like(code)
+    for t in range(terms):
+        high = conn[t : t + 1, :] // CODE_BASE
+        low = conn[t : t + 1, :] - high * CODE_BASE
+        for j in range(nsec // width):
+            code[pl.ds(j, 1), :] = high[:, j * width : (j + 1) * width].astype(F32)
+            code[pl.ds(nsec // width + j, 1), :] = low[:, j * width : (j + 1) * width].astype(F32)
+        left_out[t, classes * width :, :] = code[...].astype(BF16)
+        for q in range(classes):
+            left_out[t, q * width : (q + 1) * width, :] = matmul(order, left[t, q]).astype(BF16)
+            right_out[t, q] = matmul_nt(right[t, q], order).astype(BF16)
 
 
 def middle_kernel(classes, parts, qcol, *rest):
-    sources, (out, left, wide, sems) = rest[:-4], rest[-4:]
-    terms, nsec, width = left.shape[0], parts.shape[1], left.shape[2]
+    sources, (out, wide) = rest[:-2], rest[-2:]
+    each, nsec, width = sources[0].shape[0], parts.shape[1], sources[0].shape[2]
+    terms = each * len(sources)
     half = width // 2
-    copies = gather_copies(sources, left, sems)
     total = parts[0].astype(F32)
     for x in range(1, parts.shape[0]):
         total = total + parts[x].astype(F32)
@@ -119,11 +111,10 @@
         kept = jnp.where(qcol[...] == q, total, 0.0).astype(BF16)
         chosen.append(jnp.concatenate([kept[:, :width], kept[:, width:]], axis=0))
     for t in range(terms):
-        if t % (terms // len(copies)) == 0:
-            copies[t // (terms // len(copies))].wait()
-        image = matmul_nt(left[t, 0:width, :], chosen[0])
+        left = sources[t // each]
+        image = matmul_nt(left[t % each, 0:width, :], chosen[0])
         for q in range(1, classes):
-            image = image + matmul_nt(left[t, q * width : (q + 1) * width, :], chosen[q])
+            image = image + matmul_nt(left[t % each, q * width : (q + 1) * width, :], chosen[q])
         for j in range(4):
             ri, r = j // 2, j % 2
             wide[j, pl.ds(t, half, stride=terms), :] = image[
@@ -134,11 +125,11 @@
 
 
 def target_kernel(spread, moved, conn, qrow, dims, *rest):
-    sources, (out, right, wide, images, route, sector, sems) = rest[:-7], rest[-7:]
-    terms, classes, width = right.shape[0], right.shape[1], right.shape[2]
+    sources, (out, wide, images, route, sector) = rest[:-5], rest[-5:]
+    each, classes, width = sources[0].shape[0], sources[0].shape[1], sources[0].shape[2]
+    terms = each * len(sources)
     half, nsec = width // 2, conn.shape[1]
     blk, x = lax.axis_index("blk"), lax.axis_index("term")
-    copies = gather_copies(sources, right, sems)
     for j in range(5):
         wide[j] = moved[:, j * LANES : (j + 1) * LANES].astype(F32)
     for ih in range(2):
@@ -150,8 +141,7 @@
     classes_row = jnp.broadcast_to(qrow[...].astype(F32), (8, nsec)).astype(BF16)
     target = matmul_nt(classes_row, route[...])
     for t in range(terms):
-        if t % (terms // len(copies)) == 0:
-            copies[t // (terms // len(copies))].wait()
+        right = sources[t // each]
         both = jnp.concatenate(
             [
                 jnp.concatenate(
@@ -163,9 +153,9 @@
         ).astype(BF16)
         pick = target[0:1, t * LANES : (t + 1) * LANES]
         pick = jnp.concatenate([pick, pick], axis=1)
-        image = matmul(right[t, 0], both)
+        image = matmul(right[t % each, 0], both)
         for q in range(1, classes):
-            image = jnp.where(pick == float(q), matmul(right[t, q], both), image)
+            image = jnp.where(pick == float(q), matmul(right[t % each, q], both), image)
         high = image.astype(BF16)
         low = (image - high.astype(F32)).astype(BF16)
         for ri in range(2):
@@ -238,13 +228,9 @@
     def by_owner(a):
         return a.reshape(nblk, sec).T.reshape(nsec)
 
-    sent, left_mine, right_mine = call(
+    sent = call(
         source_kernel,
-        (
-            bf16(nblk * pairs, band * width),
-            bf16(terms, classes * width + CODE_ROWS, width),
-            bf16(terms, classes, width, width),
-        ),
+        bf16(nblk * pairs, band * width),
         [hbm] * 6,
         [
             pltpu.VMEM(psi.shape, BF16),
@@ -255,13 +241,24 @@
             pltpu.SMEM(q_row.shape, jnp.int32),
             pltpu.SMEM(d_row.shape, jnp.int32),
             pltpu.VMEM(right_env.shape, F32),
-            pltpu.VMEM((CODE_ROWS, width), F32),
             pltpu.VMEM((band * width // LANES, nblk * pairs, LANES), F32),
             pltpu.SemaphoreType.DMA((7,)),
         ],
         None,
-        (2 * pairs + 3 * terms * classes) * 2 * width**3,
+        (2 * pairs + terms * classes) * 2 * width**3,
         psi, left_env, right_env, connect, q_row, d_row,
+    )
+    left_mine, right_mine = call(
+        order_kernel,
+        (
+            bf16(terms, classes * width + CODE_ROWS, width),
+            bf16(terms, classes, width, width),
+        ),
+        [vmem] * 3,
+        [pltpu.VMEM((CODE_ROWS, width), F32)],
+        8 << 20,
+        2 * terms * classes * 2 * width**3,
+        left_env, right_env, connect,
     )
     lefts = from_all(left_mine, "term")
     rights = from_all(right_mine, "term")
@@ -294,32 +291,27 @@
     sent = call(
         functools.partial(middle_kernel, classes),
         bf16(nblk * all_terms, band * width + LANES),
-        [vmem, vmem] + [hbm] * nterm,
-        [
-            pltpu.VMEM((all_terms,) + left_mine.shape[1:], BF16),
-            pltpu.VMEM((5, nblk * all_terms, LANES), F32),
-            pltpu.SemaphoreType.DMA((nterm,)),
-        ],
-        20 << 20,
+        [vmem] * (2 + nterm),
+        [pltpu.VMEM((5, nblk * all_terms, LANES), F32)],
+        16 << 20,
         2 * all_terms * classes * width**3,
         parts, qcol, *lefts,
     )
+    sent, rights, conn_all = lax.optimization_barrier((sent, rights, conn_all))
     moved = lax.all_to_all(
         sent.reshape(nblk, all_terms, -1), "blk", split_axis=0, concat_axis=0, tiled=True
     ).reshape(nblk * all_terms, -1)
     sent = call(
         functools.partial(target_kernel, sec),
         bf16(nterm, 4 * width, kept),
-        [vmem, vmem, vmem, vmem] + [hbm] * nterm,
+        [vmem] * (4 + nterm),
         [
-            pltpu.VMEM((all_terms,) + right_mine.shape[1:], BF16),
             pltpu.VMEM((5, nblk * all_terms, LANES), F32),
             pltpu.VMEM((2, band * width, all_terms * LANES), BF16),
             pltpu.VMEM((all_terms * LANES, nsec), BF16),
             pltpu.VMEM((2, width, LANES), F32),
-            pltpu.SemaphoreType.DMA((nterm,)),
         ],
-        28 << 20,
+        24 << 20,
         2 * all_terms * (classes * width**3 + 2 * 2 * width * LANES * nsec),
         moved, conn_all, q_row, d_row, *rights,
     )

time: 199 us -> 193 us (0.970)
  blocking collectives: 18.4 us -> 91.2 us
  waiting for transfers between devices: 108 us -> 43.4 us
  starting transfers between devices: 50.3 us -> 43.1 us
  local copies, waits for them, and re-layouts: 8.18 us -> 1.65 us
    all_to_all x0 -> x1, blocking collectives: none -> 72.2 us  [on_device(): lax.all_to_all(sent.reshape(nblk, all_terms, -1), 'blk', split_axis=0, co...]
    all_to_all x1 -> x0, waiting for transfers between devices: 34.2 us -> none  [on_device(): lax.all_to_all(sent.reshape(nblk, all_terms, -1), 'blk', split_axis=0, co...]
    ppermute x6, waiting for transfers between devices: 20.4 us -> 1.47 us  [from_all(): lax.ppermute(a, axis, [(i, (i + d) % n) for i in range(n)])]
    all_to_all x1, waiting for transfers between devices: 43.4 us -> 32.5 us  [on_device(): lax.all_to_all(sent.reshape(nblk, pairs, band * width), 'blk', split_axis...]
    unnamed x23 -> x11, local copies, waits for them, and re-layouts: 6.57 us -> 0.03 us
    all_to_all x1 -> x0, starting transfers between devices: 6.38 us -> none  [on_device(): lax.all_to_all(sent.reshape(nblk, all_terms, -1), 'blk', split_axis=0, co...]
    pallas_call x4 -> x5, Pallas kernels: 11.5 us -> 10.8 us  [call(): pl.pallas_call(kernel, out_shape=out_shape, in_specs=in_specs, out_specs=...]
  transfers between devices with their start and end apart: 9 -> 8, of which waited for: 5 -> 3; matrix products, arithmetic and copies ran while one was open for 1% -> 1% of each run, Pallas kernels for 0% -> 1%
where the time goes in v3:
time: 193 us
  blocking collectives  91.2 us (47%)
  waiting for transfers between devices  43.4 us (22%)
  starting transfers between devices  43.1 us (22%)
  Pallas kernels  10.8 us (6%)
    all_to_all x1, blocking collectives, on_device(): lax.all_to_all(sent.reshape(nblk, all_terms, -1), 'blk', split_axis=0, co...  72.2 us
    all_to_all x1, waiting for transfers between devices, on_device(): lax.all_to_all(sent.reshape(nblk, pairs, band * width), 'blk', split_axis...  32.5 us
    ppermute x6, starting transfers between devices, from_all(): lax.ppermute(a, axis, [(i, (i + d) % n) for i in range(n)])  19.5 us
    all_to_all x1, starting transfers between devices, on_device(): lax.all_to_all(sent.reshape(nblk, pairs, band * width), 'blk', split_axis...  19.3 us
    all_to_all x1, blocking collectives, on_device(): lax.all_to_all(sent, 'term', split_axis=0, concat_axis=0, tiled=True)  18.9 us
    pallas_call x5, Pallas kernels, call(): pl.pallas_call(kernel, out_shape=out_shape, in_specs=in_specs, out_specs=...  10.8 us
    all_to_all x1, waiting for transfers between devices, on_device(): lax.all_to_all(total.reshape(nterm, kept, band * width), 'term', split_ax...  9.46 us
    all_to_all x1, starting transfers between devices, on_device(): lax.all_to_all(total.reshape(nterm, kept, band * width), 'term', split_ax...  4.29 us
  transfers between devices with their start and end apart: 8, of which 3 were waited for; matrix products, arithmetic and copies ran while one was open for 1% of the time, Pallas kernels for 1%

profile of v3, /device:TPU:32, one launch (start us, length us, event | category | flops | bytes accessed | tf_op | source)
XLA Modules:
  0.0 192.7 jit_solution(14386945387504684008)
XLA Ops:
  0.6 3.5 %shard_map.77 = bf16[1024,512]{1,0:T(8,128)(2,1)} custom-call(bf16[4,256,256]{2,1,0:T(8,128)(2,1)} %psi_hbm.1, bf16[2,2,256,256]{3,2,1,0:T(8,128)(2,1)} %left.1, bf16[2,2,256,256]{3,2,1,0:T(8,128)(2,1)} %right.1, s32[2,512]{1,0:T(2,128)} %conn.1, s32[1,512]{1,0:T(1,128)} %bitcast.25, s32[1,512]{1,0:T(1,128)} %bitcast.27), custom_call_target="tpu_custom_call" | custom-call | flops 671088640 | bytes 6291456 | tf_op jit(solution)/shard_map/pallas_call | solution.py:195
  4.2 0.0 copy-start
  4.2 0.0 copy-start.1
  4.2 19.3 %all-to-all-start = ((bf16[128,8,512]{2,1,0:T(8,128)(2,1)}), bf16[128,8,512]{2,1,0:T(8,128)(2,1)S(1)}, u32[]{:S(2)}, u32[]{:S(2)}) async-start(bf16[128,8,512]{2,1,0:T(8,128)(2,1)} %bitcast.29), calls=%async_computation | async-start | bytes 2097152 | tf_op jit(solution)/shard_map/all_to_all | solution.py:284
  23.6 1.3 shard_map.78
  24.9 3.4 %collective-permute-start = (bf16[2,528,256]{2,1,0:T(8,128)(2,1)S(1)}, bf16[2,528,256]{2,1,0:T(8,128)(2,1)S(1)}, u32[]{:S(2)}, u32[]{:S(2)}) collective-permute-start(bf16[2,528,256]{2,1,0:T(8,128)(2,1)S(1)} %get-tuple-element.12.rest_0_), channel_id=1, source_target_pairs={{0,1},{1,2},{2,3},{3,0},{4,5},{5,6},{6,7},{7,4},{8,9},{9,10},{10,1... | collective-permute-start | bytes 1622024 | tf_op jit(solution)/shard_map/ppermute | solution.py:208
  28.2 4.6 %collective-permute-start.1 = (bf16[2,528,256]{2,1,0:T(8,128)(2,1)S(1)}, bf16[2,528,256]{2,1,0:T(8,128)(2,1)S(1)}, u32[]{:S(2)}, u32[]{:S(2)}) collective-permute-start(bf16[2,528,256]{2,1,0:T(8,128)(2,1)S(1)} %get-tuple-element.12.rest_0_), channel_id=1, source_target_pairs={{0,2},{1,3},{2,0},{3,1},{4,6},{5,7},{6,4},{7,5},{8,10},{9,11},{10,... | collective-permute-start | bytes 1622024 | tf_op jit(solution)/shard_map/ppermute | solution.py:208
  32.9 3.3 %collective-permute-start.2 = (bf16[2,528,256]{2,1,0:T(8,128)(2,1)S(1)}, bf16[2,528,256]{2,1,0:T(8,128)(2,1)S(1)}, u32[]{:S(2)}, u32[]{:S(2)}) collective-permute-start(bf16[2,528,256]{2,1,0:T(8,128)(2,1)S(1)} %get-tuple-element.12.rest_0_), channel_id=1, source_target_pairs={{0,3},{1,0},{2,1},{3,2},{4,7},{5,4},{6,5},{7,6},{8,11},{9,8},{10,9... | collective-permute-start | bytes 1622024 | tf_op jit(solution)/shard_map/ppermute | solution.py:208
  36.2 2.5 %collective-permute-start.3 = (bf16[2,2,256,256]{3,2,1,0:T(8,128)(2,1)}, bf16[2,2,256,256]{3,2,1,0:T(8,128)(2,1)}, u32[]{:S(2)}, u32[]{:S(2)}) collective-permute-start(bf16[2,2,256,256]{3,2,1,0:T(8,128)(2,1)} %get-tuple-element.16.rest_0_), channel_id=1, source_target_pairs={{0,1},{1,2},{2,3},{3,0},{4,5},{5,6},{6,7},{7,4},{8,9},{9,10},{10,1... | collective-permute-start | bytes 1572872 | tf_op jit(solution)/shard_map/ppermute | solution.py:208
  38.8 2.8 %collective-permute-start.4 = (bf16[2,2,256,256]{3,2,1,0:T(8,128)(2,1)}, bf16[2,2,256,256]{3,2,1,0:T(8,128)(2,1)}, u32[]{:S(2)}, u32[]{:S(2)}) collective-permute-start(bf16[2,2,256,256]{3,2,1,0:T(8,128)(2,1)} %get-tuple-element.16.rest_0_), channel_id=1, source_target_pairs={{0,2},{1,3},{2,0},{3,1},{4,6},{5,7},{6,4},{7,5},{8,10},{9,11},{10,... | collective-permute-start | bytes 1572872 | tf_op jit(solution)/shard_map/ppermute | solution.py:208
  41.6 0.1 reshape.112
  41.7 0.1 reshape_squeeze.6
  41.8 0.1 copy.10
  41.9 0.1 reshape_squeeze.7
  42.0 0.1 copy.11
  42.1 0.1 copy.9
  42.2 1.5 collective-permute-done.rest_1_
  43.7 2.9 %collective-permute-start.5 = (bf16[2,2,256,256]{3,2,1,0:T(8,128)(2,1)}, bf16[2,2,256,256]{3,2,1,0:T(8,128)(2,1)}, u32[]{:S(2)}, u32[]{:S(2)}) collective-permute-start(bf16[2,2,256,256]{3,2,1,0:T(8,128)(2,1)} %get-tuple-element.16.rest_0_), channel_id=1, source_target_pairs={{0,3},{1,0},{2,1},{3,2},{4,7},{5,4},{6,5},{7,6},{8,11},{9,8},{10,9... | collective-permute-start | bytes 1572872 | tf_op jit(solution)/shard_map/ppermute | solution.py:208
  46.5 32.5 %all-to-all-done = bf16[128,8,512]{2,1,0:T(8,128)(2,1)S(1)} async-done(((bf16[128,8,512]{2,1,0:T(8,128)(2,1)}), bf16[128,8,512]{2,1,0:T(8,128)(2,1)S(1)}, u32[]{:S(2)}, u32[]{:S(2)}) %all-to-all-start) | async-done | bytes 1048608 | tf_op jit(solution)/shard_map/all_to_all | solution.py:284
  79.0 1.6 fusion.2
  80.6 4.3 %all-to-all-start.1 = ((bf16[4,128,512]{2,1,0:T(8,128)(2,1)}), bf16[4,128,512]{2,1,0:T(8,128)(2,1)S(1)}, u32[]{:S(2)}, u32[]{:S(2)}) async-start(bf16[4,128,512]{2,1,0:T(8,128)(2,1)} %bitcast.30), calls=%async_computation.1 | async-start | bytes 1048576 | tf_op jit(solution)/shard_map/all_to_all | solution.py:288
  84.8 0.1 reshape.116
  85.0 0.1 copy.12
  85.0 0.1 dynamic-slice_bitcast_fusion
  85.1 0.1 copy.13.qcol
  85.3 9.5 %all-to-all-done.1.parts = bf16[4,128,512]{2,1,0:T(8,128)(2,1)S(1)} async-done(((bf16[4,128,512]{2,1,0:T(8,128)(2,1)}), bf16[4,128,512]{2,1,0:T(8,128)(2,1)S(1)}, u32[]{:S(2)}, u32[]{:S(2)}) %all-to-all-start.1) | async-done | bytes 524320 | tf_op jit(solution)/shard_map/all_to_all | solution.py:288
  94.8 1.1 shard_map.79
  95.9 72.2 %all_to_all.20 = bf16[128,8,640]{2,1,0:T(8,128)(2,1)S(1)} all-to-all(bf16[128,8,640]{2,1,0:T(8,128)(2,1)S(1)} %bitcast.22), channel_id=1, replica_groups=mesh['blk'=128,'term'=4] {'blk'}, dimensions={0} | all-to-all | bytes 2621440 | tf_op jit(solution)/shard_map/all_to_all | solution.py:301
  168.2 4.0 %shard_map.80 = bf16[4,1024,128]{2,1,0:T(8,128)(2,1)S(1)} custom-call(bf16[1024,640]{1,0:T(8,128)(2,1)S(1)} %bitcast.23, s32[8,512]{1,0:T(8,128)S(1)} %bitcast.24, s32[1,512]{1,0:T(1,128)S(1)} %bitcast.26, s32[1,512]{1,0:T(1,128)S(1)} %bitcast.28, bf16[2,2,256,256]{3,2,1,0:T(8,128)(2,1)} %get-tuple-element.16.rest_0_, ...), custom_call_target="tpu_custom_call" | custom-call | flops 1610612736 | bytes 6291456 | tf_op jit(solution)/shard_map/pallas_call | solution.py:195
  172.1 18.9 %all_to_all.21.parts = bf16[4,1024,128]{2,1,0:T(8,128)(2,1)S(1)} all-to-all(bf16[4,1024,128]{2,1,0:T(8,128)(2,1)S(1)} %shard_map.80), channel_id=1, replica_groups=mesh['blk'=128,'term'=4] {'term'}, dimensions={0} | all-to-all | bytes 2097152 | tf_op jit(solution)/shard_map/all_to_all | solution.py:318
  191.0 0.9 shard_map.81
  192.0 0.7 reshape.120
  (23 shorter events, 0.1 us)
Async XLA Ops:
  4.2 19.4 %copy-start = (bf16[2,2,256,256]{3,2,1,0:T(8,128)(2,1)S(1)}, bf16[2,2,256,256]{3,2,1,0:T(8,128)(2,1)}, u32[]{:S(2)}) copy-start(bf16[2,2,256,256]{3,2,1,0:T(8,128)(2,1)} %left.1) | copy-start | bytes 1572868
  4.2 19.4 %copy-start.1 = (bf16[2,2,256,256]{3,2,1,0:T(8,128)(2,1)S(1)}, bf16[2,2,256,256]{3,2,1,0:T(8,128)(2,1)}, u32[]{:S(2)}) copy-start(bf16[2,2,256,256]{3,2,1,0:T(8,128)(2,1)} %right.1) | copy-start | bytes 1572868
  4.2 19.4 %copy-start.2 = (s32[2,512]{1,0:T(2,128)S(1)}, s32[2,512]{1,0:T(2,128)}, u32[]{:S(2)}) copy-start(s32[2,512]{1,0:T(2,128)} %conn.1) | copy-start | bytes 12292
  4.2 37.4 %copy-start.4 = (s32[512]{0:T(512)S(1)}, s32[512]{0:T(512)}, u32[]{:S(2)}) copy-start(s32[512]{0:T(512)} %param.11) | copy-start | bytes 6148
  4.2 74.8 %all-to-all-start = ((bf16[128,8,512]{2,1,0:T(8,128)(2,1)}), bf16[128,8,512]{2,1,0:T(8,128)(2,1)S(1)}, u32[]{:S(2)}, u32[]{:S(2)}) async-start(bf16[128,8,512]{2,1,0:T(8,128)(2,1)} %bitcast.29), calls=%async_computation | async-start | bytes 2097152 | tf_op jit(solution)/shard_map/all_to_all | solution.py:284
  24.9 18.8 %collective-permute-start = (bf16[2,528,256]{2,1,0:T(8,128)(2,1)S(1)}, bf16[2,528,256]{2,1,0:T(8,128)(2,1)S(1)}, u32[]{:S(2)}, u32[]{:S(2)}) collective-permute-start(bf16[2,528,256]{2,1,0:T(8,128)(2,1)S(1)} %get-tuple-element.12.rest_0_), channel_id=1, source_target_pairs={{0,1},{1,2},{2,3},{3,0},{4,5},{5,6},{6,7},{7,4},{8,9},{9,10},{10,1... | collective-permute-start | bytes 1622024 | tf_op jit(solution)/shard_map/ppermute | solution.py:208
  28.2 57.0 %collective-permute-start.1 = (bf16[2,528,256]{2,1,0:T(8,128)(2,1)S(1)}, bf16[2,528,256]{2,1,0:T(8,128)(2,1)S(1)}, u32[]{:S(2)}, u32[]{:S(2)}) collective-permute-start(bf16[2,528,256]{2,1,0:T(8,128)(2,1)S(1)} %get-tuple-element.12.rest_0_), channel_id=1, source_target_pairs={{0,2},{1,3},{2,0},{3,1},{4,6},{5,7},{6,4},{7,5},{8,10},{9,11},{10,... | collective-permute-start | bytes 1622024 | tf_op jit(solution)/shard_map/ppermute | solution.py:208
  32.9 52.4 %collective-permute-start.2 = (bf16[2,528,256]{2,1,0:T(8,128)(2,1)S(1)}, bf16[2,528,256]{2,1,0:T(8,128)(2,1)S(1)}, u32[]{:S(2)}, u32[]{:S(2)}) collective-permute-start(bf16[2,528,256]{2,1,0:T(8,128)(2,1)S(1)} %get-tuple-element.12.rest_0_), channel_id=1, source_target_pairs={{0,3},{1,0},{2,1},{3,2},{4,7},{5,4},{6,5},{7,6},{8,11},{9,8},{10,9... | collective-permute-start | bytes 1622024 | tf_op jit(solution)/shard_map/ppermute | solution.py:208
  36.2 59.6 %collective-permute-start.3 = (bf16[2,2,256,256]{3,2,1,0:T(8,128)(2,1)}, bf16[2,2,256,256]{3,2,1,0:T(8,128)(2,1)}, u32[]{:S(2)}, u32[]{:S(2)}) collective-permute-start(bf16[2,2,256,256]{3,2,1,0:T(8,128)(2,1)} %get-tuple-element.16.rest_0_), channel_id=1, source_target_pairs={{0,1},{1,2},{2,3},{3,0},{4,5},{5,6},{6,7},{7,4},{8,9},{9,10},{10,1... | collective-permute-start | bytes 1572872 | tf_op jit(solution)/shard_map/ppermute | solution.py:208
  38.8 57.1 %collective-permute-start.4 = (bf16[2,2,256,256]{3,2,1,0:T(8,128)(2,1)}, bf16[2,2,256,256]{3,2,1,0:T(8,128)(2,1)}, u32[]{:S(2)}, u32[]{:S(2)}) collective-permute-start(bf16[2,2,256,256]{3,2,1,0:T(8,128)(2,1)} %get-tuple-element.16.rest_0_), channel_id=1, source_target_pairs={{0,2},{1,3},{2,0},{3,1},{4,6},{5,7},{6,4},{7,5},{8,10},{9,11},{10,... | collective-permute-start | bytes 1572872 | tf_op jit(solution)/shard_map/ppermute | solution.py:208
  43.7 52.3 %collective-permute-start.5 = (bf16[2,2,256,256]{3,2,1,0:T(8,128)(2,1)}, bf16[2,2,256,256]{3,2,1,0:T(8,128)(2,1)}, u32[]{:S(2)}, u32[]{:S(2)}) collective-permute-start(bf16[2,2,256,256]{3,2,1,0:T(8,128)(2,1)} %get-tuple-element.16.rest_0_), channel_id=1, source_target_pairs={{0,3},{1,0},{2,1},{3,2},{4,7},{5,4},{6,5},{7,6},{8,11},{9,8},{10,9... | collective-permute-start | bytes 1572872 | tf_op jit(solution)/shard_map/ppermute | solution.py:208
  79.0 5.9 %copy-start.3 = (s32[512]{0:T(512)S(1)}, s32[512]{0:T(512)}, u32[]{:S(2)}) copy-start(s32[512]{0:T(512)} %param.10) | copy-start | bytes 6148
  80.6 14.2 %all-to-all-start.1 = ((bf16[4,128,512]{2,1,0:T(8,128)(2,1)}), bf16[4,128,512]{2,1,0:T(8,128)(2,1)S(1)}, u32[]{:S(2)}, u32[]{:S(2)}) async-start(bf16[4,128,512]{2,1,0:T(8,128)(2,1)} %bitcast.30), calls=%async_computation.1 | async-start | bytes 1048576 | tf_op jit(solution)/shard_map/all_to_all | solution.py:288

commit v4 on v3

--- a/solution.py
+++ b/solution.py
@@ -8,6 +8,7 @@
 from jax.sharding import PartitionSpec as P
 
 LANES = 128
+ROWS = 4
 CODE_ROWS = 16
 CODE_BASE = 16
 F32, BF16 = jnp.float32, jnp.bfloat16
@@ -102,10 +103,8 @@
     total = parts[0].astype(F32)
     for x in range(1, parts.shape[0]):
         total = total + parts[x].astype(F32)
-    for j in range(total.shape[1] // LANES):
-        wide[4, pl.ds(j, nsec, stride=terms), :] = total[:, j * LANES : (j + 1) * LANES]
-    for j in range(total.shape[1] // LANES, terms):
-        wide[4, pl.ds(j, nsec, stride=terms), :] = jnp.zeros((nsec, LANES), F32)
+    for j in range(ROWS):
+        wide[wide.shape[0] - 1, pl.ds(j, nsec, stride=ROWS), :] = total[:, j * LANES : (j + 1) * LANES]
     chosen = []
     for q in range(classes):
         kept = jnp.where(qcol[...] == q, total, 0.0).astype(BF16)
@@ -117,11 +116,11 @@
             image = image + matmul_nt(left[t % each, q * width : (q + 1) * width, :], chosen[q])
         for j in range(4):
             ri, r = j // 2, j % 2
-            wide[j, pl.ds(t, half, stride=terms), :] = image[
+            wide[4 * (t // ROWS) + j, pl.ds(t % ROWS, half, stride=ROWS), :] = image[
                 ri * half : (ri + 1) * half, r * nsec : (r + 1) * nsec
             ]
-    for j in range(5):
-        out[:, j * LANES : (j + 1) * LANES] = wide[j].astype(BF16)
+    for j in range(wide.shape[0]):
+        out[:, :, j * LANES : (j + 1) * LANES] = wide[j].reshape(half, ROWS, LANES).astype(BF16)
 
 
 def target_kernel(spread, moved, conn, qrow, dims, *rest):
@@ -130,11 +129,11 @@
     terms = each * len(sources)
     half, nsec = width // 2, conn.shape[1]
     blk, x = lax.axis_index("blk"), lax.axis_index("term")
-    for j in range(5):
-        wide[j] = moved[:, j * LANES : (j + 1) * LANES].astype(F32)
+    for j in range(wide.shape[0]):
+        wide[j] = moved[:, :, j * LANES : (j + 1) * LANES].astype(F32).reshape(half * ROWS, LANES)
     for ih in range(2):
         for r in range(2):
-            sector[ih, pl.ds(r, half, stride=2), :] = wide[4, pl.ds(2 * r + ih, half, stride=terms), :]
+            sector[ih, pl.ds(r, half, stride=2), :] = wide[wide.shape[0] - 1, pl.ds(2 * r + ih, half, stride=ROWS), :]
     source = iota((LANES, nsec), 0) * spread + x
     for t in range(terms):
         route[t * LANES : (t + 1) * LANES, :] = (conn[t : t + 1, :] == source).astype(F32).astype(BF16)
@@ -145,7 +144,11 @@
         both = jnp.concatenate(
             [
                 jnp.concatenate(
-                    [wide[2 * ri + r, pl.ds(t, half, stride=terms), :] for r in range(2)], axis=0
+                    [
+                        wide[4 * (t // ROWS) + 2 * ri + r, pl.ds(t % ROWS, half, stride=ROWS), :]
+                        for r in range(2)
+                    ],
+                    axis=0,
                 )
                 for ri in range(2)
             ],
@@ -177,12 +180,18 @@
                 out[to, first : first + LANES, :] = turned[ih][:, lh * LANES : (lh + 1) * LANES]
 
 
-def last_kernel(parts, one, two):
+def last_kernel(parts, one, two, rows):
     width = one.shape[1]
     total = parts[0, : 2 * width, :].astype(F32)
     for x in range(1, parts.shape[0]):
         total = total + parts[x, : 2 * width, :].astype(F32)
-    two[...] = total.T.astype(BF16)
+    total = total.T
+    kept = total.shape[0]
+    for j in range(2 * width // LANES):
+        ri, at = j // (width // LANES), j % (width // LANES)
+        rows[at, pl.ds(ri, kept, stride=2), :] = total[:, j * LANES : (j + 1) * LANES]
+    for at in range(width // LANES):
+        two[:, :, at * LANES : (at + 1) * LANES] = rows[at].reshape(kept, 2, LANES).astype(BF16)
     for x in range(parts.shape[0]):
         for lh in range(2):
             one[x, :, lh * LANES : (lh + 1) * LANES] = parts[
@@ -218,6 +227,7 @@
     pairs = terms * sec
     kept = nsec // nterm
     all_terms = terms * nterm
+    slots = all_terms // ROWS * band * band + 1
     blk = lax.axis_index("blk")
     x = lax.axis_index("term")
     vmem = pl.BlockSpec(memory_space=pltpu.VMEM)
@@ -290,23 +300,21 @@
     )
     sent = call(
         functools.partial(middle_kernel, classes),
-        bf16(nblk * all_terms, band * width + LANES),
+        bf16(nblk, ROWS, slots * LANES),
         [vmem] * (2 + nterm),
-        [pltpu.VMEM((5, nblk * all_terms, LANES), F32)],
+        [pltpu.VMEM((slots, nblk * ROWS, LANES), F32)],
         16 << 20,
         2 * all_terms * classes * width**3,
         parts, qcol, *lefts,
     )
     sent, rights, conn_all = lax.optimization_barrier((sent, rights, conn_all))
-    moved = lax.all_to_all(
-        sent.reshape(nblk, all_terms, -1), "blk", split_axis=0, concat_axis=0, tiled=True
-    ).reshape(nblk * all_terms, -1)
+    moved = lax.all_to_all(sent, "blk", split_axis=0, concat_axis=0, tiled=True)
     sent = call(
         functools.partial(target_kernel, sec),
         bf16(nterm, 4 * width, kept),
         [vmem] * (4 + nterm),
         [
-            pltpu.VMEM((5, nblk * all_terms, LANES), F32),
+            pltpu.VMEM((slots, nblk * ROWS, LANES), F32),
             pltpu.VMEM((2, band * width, all_terms * LANES), BF16),
             pltpu.VMEM((all_terms * LANES, nsec), BF16),
             pltpu.VMEM((2, width, LANES), F32),
@@ -318,14 +326,14 @@
     parts = lax.all_to_all(sent, "term", split_axis=0, concat_axis=0, tiled=True)
     sigma_one, two = call(
         last_kernel,
-        (bf16(sec, width, width), bf16(kept, band * width)),
+        (bf16(sec, width, width), bf16(kept, band, width)),
         [vmem],
-        [],
+        [pltpu.VMEM((width // LANES, kept * band, LANES), F32)],
         16 << 20,
         0,
         parts,
     )
-    return (sigma_one, two.reshape(kept, band, width))
+    return (sigma_one, two)
 
 
 def solution(mesh):

time: 193 us -> 187 us (0.969)
  blocking collectives: 91.2 us -> 86 us
    all_to_all x1, blocking collectives: 72.2 us -> 67 us  [on_device(): moved = lax.all_to_all(sent, 'blk', split_axis=0, concat_axis=0, tiled=True)]
where the time goes in v4:
time: 187 us
  blocking collectives  86 us (46%)
  waiting for transfers between devices  43.4 us (23%)
  starting transfers between devices  43.1 us (23%)
  Pallas kernels  10.9 us (6%)
    all_to_all x1, blocking collectives, on_device(): moved = lax.all_to_all(sent, 'blk', split_axis=0, concat_axis=0, tiled=True)  67 us
    all_to_all x1, waiting for transfers between devices, on_device(): lax.all_to_all(sent.reshape(nblk, pairs, band * width), 'blk', split_axis...  32.5 us
    ppermute x6, starting transfers between devices, from_all(): lax.ppermute(a, axis, [(i, (i + d) % n) for i in range(n)])  19.5 us
    all_to_all x1, starting transfers between devices, on_device(): lax.all_to_all(sent.reshape(nblk, pairs, band * width), 'blk', split_axis...  19.3 us
    all_to_all x1, blocking collectives, on_device(): lax.all_to_all(sent, 'term', split_axis=0, concat_axis=0, tiled=True)  19 us
    pallas_call x5, Pallas kernels, call(): pl.pallas_call(kernel, out_shape=out_shape, in_specs=in_specs, out_specs=...  10.9 us
    all_to_all x1, waiting for transfers between devices, on_device(): lax.all_to_all(total.reshape(nterm, kept, band * width), 'term', split_ax...  9.46 us
    all_to_all x1, starting transfers between devices, on_device(): lax.all_to_all(total.reshape(nterm, kept, band * width), 'term', split_ax...  4.29 us
  transfers between devices with their start and end apart: 8, of which 3 were waited for; matrix products, arithmetic and copies ran while one was open for 1% of the time, Pallas kernels for 1%

profile of v4, /device:TPU:32, one launch (start us, length us, event | category | flops | bytes accessed | tf_op | source)
XLA Modules:
  0.0 186.9 jit_solution(8019409901917612588)
XLA Ops:
  0.6 3.5 %shard_map.77 = bf16[1024,512]{1,0:T(8,128)(2,1)} custom-call(bf16[4,256,256]{2,1,0:T(8,128)(2,1)} %psi_hbm.1, bf16[2,2,256,256]{3,2,1,0:T(8,128)(2,1)} %left.1, bf16[2,2,256,256]{3,2,1,0:T(8,128)(2,1)} %right.1, s32[2,512]{1,0:T(2,128)} %conn.1, s32[1,512]{1,0:T(1,128)} %bitcast.21, s32[1,512]{1,0:T(1,128)} %bitcast.23), custom_call_target="tpu_custom_call" | custom-call | flops 671088640 | bytes 6291456 | tf_op jit(solution)/shard_map/pallas_call | solution.py:204
  4.2 0.0 copy-start
  4.2 0.0 copy-start.2
  4.2 0.0 copy-start.4
  4.2 19.3 %all-to-all-start = ((bf16[128,8,512]{2,1,0:T(8,128)(2,1)}), bf16[128,8,512]{2,1,0:T(8,128)(2,1)S(1)}, u32[]{:S(2)}, u32[]{:S(2)}) async-start(bf16[128,8,512]{2,1,0:T(8,128)(2,1)} %bitcast.25), calls=%async_computation | async-start | bytes 2097152 | tf_op jit(solution)/shard_map/all_to_all | solution.py:294
  23.6 1.3 shard_map.78
  24.8 3.4 %collective-permute-start = (bf16[2,528,256]{2,1,0:T(8,128)(2,1)S(1)}, bf16[2,528,256]{2,1,0:T(8,128)(2,1)S(1)}, u32[]{:S(2)}, u32[]{:S(2)}) collective-permute-start(bf16[2,528,256]{2,1,0:T(8,128)(2,1)S(1)} %get-tuple-element.10.rest_0_), channel_id=1, source_target_pairs={{0,1},{1,2},{2,3},{3,0},{4,5},{5,6},{6,7},{7,4},{8,9},{9,10},{10,1... | collective-permute-start | bytes 1622024 | tf_op jit(solution)/shard_map/ppermute | solution.py:217
  28.2 4.6 %collective-permute-start.1 = (bf16[2,528,256]{2,1,0:T(8,128)(2,1)S(1)}, bf16[2,528,256]{2,1,0:T(8,128)(2,1)S(1)}, u32[]{:S(2)}, u32[]{:S(2)}) collective-permute-start(bf16[2,528,256]{2,1,0:T(8,128)(2,1)S(1)} %get-tuple-element.10.rest_0_), channel_id=1, source_target_pairs={{0,2},{1,3},{2,0},{3,1},{4,6},{5,7},{6,4},{7,5},{8,10},{9,11},{10,... | collective-permute-start | bytes 1622024 | tf_op jit(solution)/shard_map/ppermute | solution.py:217
  32.9 3.3 %collective-permute-start.2 = (bf16[2,528,256]{2,1,0:T(8,128)(2,1)S(1)}, bf16[2,528,256]{2,1,0:T(8,128)(2,1)S(1)}, u32[]{:S(2)}, u32[]{:S(2)}) collective-permute-start(bf16[2,528,256]{2,1,0:T(8,128)(2,1)S(1)} %get-tuple-element.10.rest_0_), channel_id=1, source_target_pairs={{0,3},{1,0},{2,1},{3,2},{4,7},{5,4},{6,5},{7,6},{8,11},{9,8},{10,9... | collective-permute-start | bytes 1622024 | tf_op jit(solution)/shard_map/ppermute | solution.py:217
  36.2 2.5 %collective-permute-start.3 = (bf16[2,2,256,256]{3,2,1,0:T(8,128)(2,1)}, bf16[2,2,256,256]{3,2,1,0:T(8,128)(2,1)}, u32[]{:S(2)}, u32[]{:S(2)}) collective-permute-start(bf16[2,2,256,256]{3,2,1,0:T(8,128)(2,1)} %get-tuple-element.14.rest_0_), channel_id=1, source_target_pairs={{0,1},{1,2},{2,3},{3,0},{4,5},{5,6},{6,7},{7,4},{8,9},{9,10},{10,1... | collective-permute-start | bytes 1572872 | tf_op jit(solution)/shard_map/ppermute | solution.py:217
  38.7 2.8 %collective-permute-start.4 = (bf16[2,2,256,256]{3,2,1,0:T(8,128)(2,1)}, bf16[2,2,256,256]{3,2,1,0:T(8,128)(2,1)}, u32[]{:S(2)}, u32[]{:S(2)}) collective-permute-start(bf16[2,2,256,256]{3,2,1,0:T(8,128)(2,1)} %get-tuple-element.14.rest_0_), channel_id=1, source_target_pairs={{0,2},{1,3},{2,0},{3,1},{4,6},{5,7},{6,4},{7,5},{8,10},{9,11},{10,... | collective-permute-start | bytes 1572872 | tf_op jit(solution)/shard_map/ppermute | solution.py:217
  41.6 0.1 reshape.103
  41.7 0.1 reshape_squeeze.6
  41.8 0.1 copy.10
  41.9 0.1 reshape_squeeze.7
  42.0 0.1 copy.11
  42.1 0.1 copy.9
  42.2 1.5 collective-permute-done.rest_1_
  43.6 2.9 %collective-permute-start.5 = (bf16[2,2,256,256]{3,2,1,0:T(8,128)(2,1)}, bf16[2,2,256,256]{3,2,1,0:T(8,128)(2,1)}, u32[]{:S(2)}, u32[]{:S(2)}) collective-permute-start(bf16[2,2,256,256]{3,2,1,0:T(8,128)(2,1)} %get-tuple-element.14.rest_0_), channel_id=1, source_target_pairs={{0,3},{1,0},{2,1},{3,2},{4,7},{5,4},{6,5},{7,6},{8,11},{9,8},{10,9... | collective-permute-start | bytes 1572872 | tf_op jit(solution)/shard_map/ppermute | solution.py:217
  46.5 32.5 %all-to-all-done = bf16[128,8,512]{2,1,0:T(8,128)(2,1)S(1)} async-done(((bf16[128,8,512]{2,1,0:T(8,128)(2,1)}), bf16[128,8,512]{2,1,0:T(8,128)(2,1)S(1)}, u32[]{:S(2)}, u32[]{:S(2)}) %all-to-all-start) | async-done | bytes 1048608 | tf_op jit(solution)/shard_map/all_to_all | solution.py:294
  79.0 1.6 fusion.2
  80.6 4.3 %all-to-all-start.1 = ((bf16[4,128,512]{2,1,0:T(8,128)(2,1)}), bf16[4,128,512]{2,1,0:T(8,128)(2,1)S(1)}, u32[]{:S(2)}, u32[]{:S(2)}) async-start(bf16[4,128,512]{2,1,0:T(8,128)(2,1)} %bitcast.26), calls=%async_computation.1 | async-start | bytes 1048576 | tf_op jit(solution)/shard_map/all_to_all | solution.py:298
  84.8 0.1 reshape.107
  85.0 0.1 copy.12
  85.0 0.1 dynamic-slice_bitcast_fusion
  85.1 0.1 copy.13.qcol
  85.3 9.5 %all-to-all-done.1.parts = bf16[4,128,512]{2,1,0:T(8,128)(2,1)S(1)} async-done(((bf16[4,128,512]{2,1,0:T(8,128)(2,1)}), bf16[4,128,512]{2,1,0:T(8,128)(2,1)S(1)}, u32[]{:S(2)}, u32[]{:S(2)}) %all-to-all-start.1) | async-done | bytes 524320 | tf_op jit(solution)/shard_map/all_to_all | solution.py:298
  94.8 1.0 shard_map.79
  95.8 67.0 %all_to_all.20.moved = bf16[128,4,1152]{2,1,0:T(4,128)(2,1)S(1)} all-to-all(bf16[128,4,1152]{2,1,0:T(4,128)(2,1)S(1)} %shard_map.79), channel_id=1, replica_groups=mesh['blk'=128,'term'=4] {'blk'}, dimensions={0} | all-to-all | bytes 2359296 | tf_op jit(solution)/shard_map/all_to_all | solution.py:311
  162.8 4.0 %shard_map.80 = bf16[4,1024,128]{2,1,0:T(8,128)(2,1)S(1)} custom-call(bf16[128,4,1152]{2,1,0:T(4,128)(2,1)S(1)} %all_to_all.20.moved, s32[8,512]{1,0:T(8,128)S(1)} %bitcast.20, s32[1,512]{1,0:T(1,128)S(1)} %bitcast.22, s32[1,512]{1,0:T(1,128)S(1)} %bitcast.24, bf16[2,2,256,256]{3,2,1,0:T(8,128)(2,1)} %get-tuple-element.14.rest_0_, ...), custom_call_target="tpu_custom_call" | custom-call | flops 1610612736 | bytes 6291456 | tf_op jit(solution)/shard_map/pallas_call | solution.py:204
  166.9 19.0 %all_to_all.21.parts = bf16[4,1024,128]{2,1,0:T(8,128)(2,1)S(1)} all-to-all(bf16[4,1024,128]{2,1,0:T(8,128)(2,1)S(1)} %shard_map.80), channel_id=1, replica_groups=mesh['blk'=128,'term'=4] {'term'}, dimensions={0} | all-to-all | bytes 2097152 | tf_op jit(solution)/shard_map/all_to_all | solution.py:326
  185.8 1.1 shard_map.81
  (22 shorter events, 0.1 us)
Async XLA Ops:
  4.2 19.4 %copy-start = (bf16[2,2,256,256]{3,2,1,0:T(8,128)(2,1)S(1)}, bf16[2,2,256,256]{3,2,1,0:T(8,128)(2,1)}, u32[]{:S(2)}) copy-start(bf16[2,2,256,256]{3,2,1,0:T(8,128)(2,1)} %left.1) | copy-start | bytes 1572868
  4.2 19.4 %copy-start.1 = (bf16[2,2,256,256]{3,2,1,0:T(8,128)(2,1)S(1)}, bf16[2,2,256,256]{3,2,1,0:T(8,128)(2,1)}, u32[]{:S(2)}) copy-start(bf16[2,2,256,256]{3,2,1,0:T(8,128)(2,1)} %right.1) | copy-start | bytes 1572868
  4.2 19.4 %copy-start.2 = (s32[2,512]{1,0:T(2,128)S(1)}, s32[2,512]{1,0:T(2,128)}, u32[]{:S(2)}) copy-start(s32[2,512]{1,0:T(2,128)} %conn.1) | copy-start | bytes 12292
  4.2 37.3 %copy-start.4 = (s32[512]{0:T(512)S(1)}, s32[512]{0:T(512)}, u32[]{:S(2)}) copy-start(s32[512]{0:T(512)} %param.11) | copy-start | bytes 6148
  4.2 74.8 %all-to-all-start = ((bf16[128,8,512]{2,1,0:T(8,128)(2,1)}), bf16[128,8,512]{2,1,0:T(8,128)(2,1)S(1)}, u32[]{:S(2)}, u32[]{:S(2)}) async-start(bf16[128,8,512]{2,1,0:T(8,128)(2,1)} %bitcast.25), calls=%async_computation | async-start | bytes 2097152 | tf_op jit(solution)/shard_map/all_to_all | solution.py:294
  24.8 18.8 %collective-permute-start = (bf16[2,528,256]{2,1,0:T(8,128)(2,1)S(1)}, bf16[2,528,256]{2,1,0:T(8,128)(2,1)S(1)}, u32[]{:S(2)}, u32[]{:S(2)}) collective-permute-start(bf16[2,528,256]{2,1,0:T(8,128)(2,1)S(1)} %get-tuple-element.10.rest_0_), channel_id=1, source_target_pairs={{0,1},{1,2},{2,3},{3,0},{4,5},{5,6},{6,7},{7,4},{8,9},{9,10},{10,1... | collective-permute-start | bytes 1622024 | tf_op jit(solution)/shard_map/ppermute | solution.py:217
  28.2 57.0 %collective-permute-start.1 = (bf16[2,528,256]{2,1,0:T(8,128)(2,1)S(1)}, bf16[2,528,256]{2,1,0:T(8,128)(2,1)S(1)}, u32[]{:S(2)}, u32[]{:S(2)}) collective-permute-start(bf16[2,528,256]{2,1,0:T(8,128)(2,1)S(1)} %get-tuple-element.10.rest_0_), channel_id=1, source_target_pairs={{0,2},{1,3},{2,0},{3,1},{4,6},{5,7},{6,4},{7,5},{8,10},{9,11},{10,... | collective-permute-start | bytes 1622024 | tf_op jit(solution)/shard_map/ppermute | solution.py:217
  32.9 52.4 %collective-permute-start.2 = (bf16[2,528,256]{2,1,0:T(8,128)(2,1)S(1)}, bf16[2,528,256]{2,1,0:T(8,128)(2,1)S(1)}, u32[]{:S(2)}, u32[]{:S(2)}) collective-permute-start(bf16[2,528,256]{2,1,0:T(8,128)(2,1)S(1)} %get-tuple-element.10.rest_0_), channel_id=1, source_target_pairs={{0,3},{1,0},{2,1},{3,2},{4,7},{5,4},{6,5},{7,6},{8,11},{9,8},{10,9... | collective-permute-start | bytes 1622024 | tf_op jit(solution)/shard_map/ppermute | solution.py:217
  36.2 59.6 %collective-permute-start.3 = (bf16[2,2,256,256]{3,2,1,0:T(8,128)(2,1)}, bf16[2,2,256,256]{3,2,1,0:T(8,128)(2,1)}, u32[]{:S(2)}, u32[]{:S(2)}) collective-permute-start(bf16[2,2,256,256]{3,2,1,0:T(8,128)(2,1)} %get-tuple-element.14.rest_0_), channel_id=1, source_target_pairs={{0,1},{1,2},{2,3},{3,0},{4,5},{5,6},{6,7},{7,4},{8,9},{9,10},{10,1... | collective-permute-start | bytes 1572872 | tf_op jit(solution)/shard_map/ppermute | solution.py:217
  38.7 57.1 %collective-permute-start.4 = (bf16[2,2,256,256]{3,2,1,0:T(8,128)(2,1)}, bf16[2,2,256,256]{3,2,1,0:T(8,128)(2,1)}, u32[]{:S(2)}, u32[]{:S(2)}) collective-permute-start(bf16[2,2,256,256]{3,2,1,0:T(8,128)(2,1)} %get-tuple-element.14.rest_0_), channel_id=1, source_target_pairs={{0,2},{1,3},{2,0},{3,1},{4,6},{5,7},{6,4},{7,5},{8,10},{9,11},{10,... | collective-permute-start | bytes 1572872 | tf_op jit(solution)/shard_map/ppermute | solution.py:217
  43.6 52.2 %collective-permute-start.5 = (bf16[2,2,256,256]{3,2,1,0:T(8,128)(2,1)}, bf16[2,2,256,256]{3,2,1,0:T(8,128)(2,1)}, u32[]{:S(2)}, u32[]{:S(2)}) collective-permute-start(bf16[2,2,256,256]{3,2,1,0:T(8,128)(2,1)} %get-tuple-element.14.rest_0_), channel_id=1, source_target_pairs={{0,3},{1,0},{2,1},{3,2},{4,7},{5,4},{6,5},{7,6},{8,11},{9,8},{10,9... | collective-permute-start | bytes 1572872 | tf_op jit(solution)/shard_map/ppermute | solution.py:217
  79.0 5.9 %copy-start.3 = (s32[512]{0:T(512)S(1)}, s32[512]{0:T(512)}, u32[]{:S(2)}) copy-start(s32[512]{0:T(512)} %param.10) | copy-start | bytes 6148
  80.6 14.2 %all-to-all-start.1 = ((bf16[4,128,512]{2,1,0:T(8,128)(2,1)}), bf16[4,128,512]{2,1,0:T(8,128)(2,1)S(1)}, u32[]{:S(2)}, u32[]{:S(2)}) async-start(bf16[4,128,512]{2,1,0:T(8,128)(2,1)} %bitcast.26), calls=%async_computation.1 | async-start | bytes 1048576 | tf_op jit(solution)/shard_map/all_to_all | solution.py:298

commit v5 on v4

--- a/solution.py
+++ b/solution.py
@@ -212,9 +212,13 @@
     )(*operands)
 
 
-def from_all(a, axis):
+def from_all(a, axis, way):
     n = lax.axis_size(axis)
-    return [a] + [lax.ppermute(a, axis, [(i, (i + d) % n) for i in range(n)]) for d in range(1, n)]
+    step = lambda v, d: lax.ppermute(v, axis, [(i, (i + d) % n) for i in range(n)])
+    slots = {0: a, 1: step(a, 1), n - 1: step(a, -1)}
+    for d in range(2, n - 1):
+        slots[d] = step(slots[(d - way) % n], way)
+    return [slots[d] for d in range(n)]
 
 
 def on_device(psi, left_env, right_env, connect, qclass, sector_dims):
@@ -270,8 +274,8 @@
         2 * terms * classes * 2 * width**3,
         left_env, right_env, connect,
     )
-    lefts = from_all(left_mine, "term")
-    rights = from_all(right_mine, "term")
+    lefts = from_all(left_mine, "term", 1)
+    rights = from_all(right_mine, "term", -1)
     code = jnp.concatenate([a[:, classes * width :, :] for a in lefts], axis=0).astype(F32)
     halves = nsec // width
     conn_all = CODE_BASE * code[:, :halves].reshape(all_terms, nsec) + code[

time: 187 us -> 187 us (level)
    all_to_all x1, waiting for transfers between devices: 32.5 us -> 26.9 us  [on_device(): lax.all_to_all(sent.reshape(nblk, pairs, band * width), 'blk', split_axis...]
    ppermute x6, waiting for transfers between devices: 1.47 us -> 6.86 us  [from_all(): lax.ppermute(v, axis, [(i, (i + d) % n) for i in range(n)])]
where the time goes in v5:
time: 187 us; the launch traced here: 186 us
  blocking collectives  85.5 us (46%)
  starting transfers between devices  43.3 us (23%)
  waiting for transfers between devices  43.3 us (23%)
  Pallas kernels  10.9 us (6%)
    all_to_all x1, blocking collectives, on_device(): moved = lax.all_to_all(sent, 'blk', split_axis=0, concat_axis=0, tiled=True)  67 us
    all_to_all x1, waiting for transfers between devices, on_device(): lax.all_to_all(sent.reshape(nblk, pairs, band * width), 'blk', split_axis...  26.9 us
    ppermute x6, starting transfers between devices, from_all(): lax.ppermute(v, axis, [(i, (i + d) % n) for i in range(n)])  19.7 us
    all_to_all x1, starting transfers between devices, on_device(): lax.all_to_all(sent.reshape(nblk, pairs, band * width), 'blk', split_axis...  19.3 us
    all_to_all x1, blocking collectives, on_device(): lax.all_to_all(sent, 'term', split_axis=0, concat_axis=0, tiled=True)  18.5 us
    pallas_call x5, Pallas kernels, call(): pl.pallas_call(kernel, out_shape=out_shape, in_specs=in_specs, out_specs=...  10.9 us
    all_to_all x1, waiting for transfers between devices, on_device(): lax.all_to_all(total.reshape(nterm, kept, band * width), 'term', split_ax...  9.46 us
    ppermute x6, waiting for transfers between devices, from_all(): lax.ppermute(v, axis, [(i, (i + d) % n) for i in range(n)])  6.86 us
  transfers between devices with their start and end apart: 8, of which 3 were waited for; matrix products, arithmetic and copies ran while one was open for 1% of the time, Pallas kernels for 1%

profile of v5, /device:TPU:32, one launch (start us, length us, event | category | flops | bytes accessed | tf_op | source)
XLA Modules:
  0.0 186.4 jit_solution(17744438201071948893)
XLA Ops:
  0.6 3.5 %shard_map.77 = bf16[1024,512]{1,0:T(8,128)(2,1)} custom-call(bf16[4,256,256]{2,1,0:T(8,128)(2,1)} %psi_hbm.1, bf16[2,2,256,256]{3,2,1,0:T(8,128)(2,1)} %left.1, bf16[2,2,256,256]{3,2,1,0:T(8,128)(2,1)} %right.1, s32[2,512]{1,0:T(2,128)} %conn.1, s32[1,512]{1,0:T(1,128)} %bitcast.21, s32[1,512]{1,0:T(1,128)} %bitcast.23), custom_call_target="tpu_custom_call" | custom-call | flops 671088640 | bytes 6291456 | tf_op jit(solution)/shard_map/pallas_call | solution.py:204
  4.2 0.0 copy-start
  4.2 0.0 copy-start.2
  4.2 0.0 copy-start.4
  4.2 19.3 %all-to-all-start = ((bf16[128,8,512]{2,1,0:T(8,128)(2,1)}), bf16[128,8,512]{2,1,0:T(8,128)(2,1)S(1)}, u32[]{:S(2)}, u32[]{:S(2)}) async-start(bf16[128,8,512]{2,1,0:T(8,128)(2,1)} %bitcast.25), calls=%async_computation | async-start | bytes 2097152 | tf_op jit(solution)/shard_map/all_to_all | solution.py:298
  23.6 1.3 shard_map.78
  24.8 3.4 %collective-permute-start = (bf16[2,528,256]{2,1,0:T(8,128)(2,1)S(1)}, bf16[2,528,256]{2,1,0:T(8,128)(2,1)S(1)}, u32[]{:S(2)}, u32[]{:S(2)}) collective-permute-start(bf16[2,528,256]{2,1,0:T(8,128)(2,1)S(1)} %get-tuple-element.10.rest_0_), channel_id=1, source_target_pairs={{0,1},{1,2},{2,3},{3,0},{4,5},{5,6},{6,7},{7,4},{8,9},{9,10},{10,1... | collective-permute-start | bytes 1622024 | tf_op jit(solution)/shard_map/ppermute | solution.py:217
  28.2 3.7 %collective-permute-start.4 = (bf16[2,2,256,256]{3,2,1,0:T(8,128)(2,1)}, bf16[2,2,256,256]{3,2,1,0:T(8,128)(2,1)}, u32[]{:S(2)}, u32[]{:S(2)}) collective-permute-start(bf16[2,2,256,256]{3,2,1,0:T(8,128)(2,1)} %get-tuple-element.14.rest_0_), channel_id=1, source_target_pairs={{0,3},{1,0},{2,1},{3,2},{4,7},{5,4},{6,5},{7,6},{8,11},{9,8},{10,9... | collective-permute-start | bytes 1572872 | tf_op jit(solution)/shard_map/ppermute | solution.py:217
  31.9 3.5 %collective-permute-start.2 = (bf16[2,528,256]{2,1,0:T(8,128)(2,1)S(1)}, bf16[2,528,256]{2,1,0:T(8,128)(2,1)S(1)}, u32[]{:S(2)}, u32[]{:S(2)}) collective-permute-start(bf16[2,528,256]{2,1,0:T(8,128)(2,1)S(1)} %get-tuple-element.10.rest_0_), channel_id=1, source_target_pairs={{0,3},{1,0},{2,1},{3,2},{4,7},{5,4},{6,5},{7,6},{8,11},{9,8},{10,9... | collective-permute-start | bytes 1622024 | tf_op jit(solution)/shard_map/ppermute | solution.py:217
  35.4 2.4 %collective-permute-start.3 = (bf16[2,2,256,256]{3,2,1,0:T(8,128)(2,1)}, bf16[2,2,256,256]{3,2,1,0:T(8,128)(2,1)}, u32[]{:S(2)}, u32[]{:S(2)}) collective-permute-start(bf16[2,2,256,256]{3,2,1,0:T(8,128)(2,1)} %get-tuple-element.14.rest_0_), channel_id=1, source_target_pairs={{0,1},{1,2},{2,3},{3,0},{4,5},{5,6},{6,7},{7,4},{8,9},{9,10},{10,1... | collective-permute-start | bytes 1572872 | tf_op jit(solution)/shard_map/ppermute | solution.py:217
  37.8 0.1 reshape.103
  37.9 0.1 reshape_squeeze.6
  38.0 0.1 copy.10
  38.1 0.1 reshape_squeeze.7
  38.2 0.1 copy.11
  38.3 0.1 copy.9
  38.4 6.8 %collective-permute-done.4.rest_3_ = bf16[2,2,256,256]{3,2,1,0:T(8,128)(2,1)} collective-permute-done((bf16[2,2,256,256]{3,2,1,0:T(8,128)(2,1)}, bf16[2,2,256,256]{3,2,1,0:T(8,128)(2,1)}, u32[]{:S(2)}, u32[]{:S(2)}) %collective-permute-start.4) | collective-permute-done | bytes 524320 | tf_op jit(solution)/shard_map/ppermute | solution.py:217
  45.2 4.9 %collective-permute-start.5 = (bf16[2,2,256,256]{3,2,1,0:T(8,128)(2,1)}, bf16[2,2,256,256]{3,2,1,0:T(8,128)(2,1)}, u32[]{:S(2)}, u32[]{:S(2)}) collective-permute-start(bf16[2,2,256,256]{3,2,1,0:T(8,128)(2,1)} %collective-permute-done.4.rest_3_), channel_id=1, source_target_pairs={{0,3},{1,0},{2,1},{3,2},{4,7},{5,4},{6,5},{7,6},{8,11},{9,8},{10,9... | collective-permute-start | bytes 1572872 | tf_op jit(solution)/shard_map/ppermute | solution.py:217
  50.1 1.9 %collective-permute-start.1 = (bf16[2,528,256]{2,1,0:T(8,128)(2,1)S(1)}, bf16[2,528,256]{2,1,0:T(8,128)(2,1)S(1)}, u32[]{:S(2)}, u32[]{:S(2)}) collective-permute-start(bf16[2,528,256]{2,1,0:T(8,128)(2,1)S(1)} %collective-permute-done.rest_1_), channel_id=1, source_target_pairs={{0,1},{1,2},{2,3},{3,0},{4,5},{5,6},{6,7},{7,4},{8,9},{9,10},{10,1... | collective-permute-start | bytes 1622024 | tf_op jit(solution)/shard_map/ppermute | solution.py:217
  52.1 26.9 %all-to-all-done = bf16[128,8,512]{2,1,0:T(8,128)(2,1)S(1)} async-done(((bf16[128,8,512]{2,1,0:T(8,128)(2,1)}), bf16[128,8,512]{2,1,0:T(8,128)(2,1)S(1)}, u32[]{:S(2)}, u32[]{:S(2)}) %all-to-all-start) | async-done | bytes 1048608 | tf_op jit(solution)/shard_map/all_to_all | solution.py:298
  79.0 1.6 fusion.2
  80.6 4.3 %all-to-all-start.1 = ((bf16[4,128,512]{2,1,0:T(8,128)(2,1)}), bf16[4,128,512]{2,1,0:T(8,128)(2,1)S(1)}, u32[]{:S(2)}, u32[]{:S(2)}) async-start(bf16[4,128,512]{2,1,0:T(8,128)(2,1)} %bitcast.26), calls=%async_computation.1 | async-start | bytes 1048576 | tf_op jit(solution)/shard_map/all_to_all | solution.py:302
  84.9 0.1 reshape.107
  85.0 0.1 copy.12
  85.0 0.1 dynamic-slice_bitcast_fusion
  85.1 0.1 copy.13.qcol
  85.3 9.5 %all-to-all-done.1.parts = bf16[4,128,512]{2,1,0:T(8,128)(2,1)S(1)} async-done(((bf16[4,128,512]{2,1,0:T(8,128)(2,1)}), bf16[4,128,512]{2,1,0:T(8,128)(2,1)S(1)}, u32[]{:S(2)}, u32[]{:S(2)}) %all-to-all-start.1) | async-done | bytes 524320 | tf_op jit(solution)/shard_map/all_to_all | solution.py:302
  94.8 1.0 shard_map.79
  95.8 67.0 %all_to_all.20.moved = bf16[128,4,1152]{2,1,0:T(4,128)(2,1)S(1)} all-to-all(bf16[128,4,1152]{2,1,0:T(4,128)(2,1)S(1)} %shard_map.79), channel_id=1, replica_groups=mesh['blk'=128,'term'=4] {'blk'}, dimensions={0} | all-to-all | bytes 2359296 | tf_op jit(solution)/shard_map/all_to_all | solution.py:315
  162.8 4.0 %shard_map.80 = bf16[4,1024,128]{2,1,0:T(8,128)(2,1)S(1)} custom-call(bf16[128,4,1152]{2,1,0:T(4,128)(2,1)S(1)} %all_to_all.20.moved, s32[8,512]{1,0:T(8,128)S(1)} %bitcast.20, s32[1,512]{1,0:T(1,128)S(1)} %bitcast.22, s32[1,512]{1,0:T(1,128)S(1)} %bitcast.24, bf16[2,2,256,256]{3,2,1,0:T(8,128)(2,1)} %get-tuple-element.14.rest_0_, ...), custom_call_target="tpu_custom_call" | custom-call | flops 1610612736 | bytes 6291456 | tf_op jit(solution)/shard_map/pallas_call | solution.py:204
  166.9 18.5 %all_to_all.21.parts = bf16[4,1024,128]{2,1,0:T(8,128)(2,1)S(1)} all-to-all(bf16[4,1024,128]{2,1,0:T(8,128)(2,1)S(1)} %shard_map.80), channel_id=1, replica_groups=mesh['blk'=128,'term'=4] {'term'}, dimensions={0} | all-to-all | bytes 2097152 | tf_op jit(solution)/shard_map/all_to_all | solution.py:330
  185.3 1.1 shard_map.81
  (22 shorter events, 0.1 us)
Async XLA Ops:
  4.2 19.4 %copy-start = (bf16[2,2,256,256]{3,2,1,0:T(8,128)(2,1)S(1)}, bf16[2,2,256,256]{3,2,1,0:T(8,128)(2,1)}, u32[]{:S(2)}) copy-start(bf16[2,2,256,256]{3,2,1,0:T(8,128)(2,1)} %left.1) | copy-start | bytes 1572868
  4.2 19.4 %copy-start.1 = (bf16[2,2,256,256]{3,2,1,0:T(8,128)(2,1)S(1)}, bf16[2,2,256,256]{3,2,1,0:T(8,128)(2,1)}, u32[]{:S(2)}) copy-start(bf16[2,2,256,256]{3,2,1,0:T(8,128)(2,1)} %right.1) | copy-start | bytes 1572868
  4.2 19.4 %copy-start.2 = (s32[2,512]{1,0:T(2,128)S(1)}, s32[2,512]{1,0:T(2,128)}, u32[]{:S(2)}) copy-start(s32[2,512]{1,0:T(2,128)} %conn.1) | copy-start | bytes 12292
  4.2 33.6 %copy-start.4 = (s32[512]{0:T(512)S(1)}, s32[512]{0:T(512)}, u32[]{:S(2)}) copy-start(s32[512]{0:T(512)} %param.11) | copy-start | bytes 6148
  4.2 74.8 %all-to-all-start = ((bf16[128,8,512]{2,1,0:T(8,128)(2,1)}), bf16[128,8,512]{2,1,0:T(8,128)(2,1)S(1)}, u32[]{:S(2)}, u32[]{:S(2)}) async-start(bf16[128,8,512]{2,1,0:T(8,128)(2,1)} %bitcast.25), calls=%async_computation | async-start | bytes 2097152 | tf_op jit(solution)/shard_map/all_to_all | solution.py:298
  24.8 25.3 %collective-permute-start = (bf16[2,528,256]{2,1,0:T(8,128)(2,1)S(1)}, bf16[2,528,256]{2,1,0:T(8,128)(2,1)S(1)}, u32[]{:S(2)}, u32[]{:S(2)}) collective-permute-start(bf16[2,528,256]{2,1,0:T(8,128)(2,1)S(1)} %get-tuple-element.10.rest_0_), channel_id=1, source_target_pairs={{0,1},{1,2},{2,3},{3,0},{4,5},{5,6},{6,7},{7,4},{8,9},{9,10},{10,1... | collective-permute-start | bytes 1622024 | tf_op jit(solution)/shard_map/ppermute | solution.py:217
  28.2 17.0 %collective-permute-start.4 = (bf16[2,2,256,256]{3,2,1,0:T(8,128)(2,1)}, bf16[2,2,256,256]{3,2,1,0:T(8,128)(2,1)}, u32[]{:S(2)}, u32[]{:S(2)}) collective-permute-start(bf16[2,2,256,256]{3,2,1,0:T(8,128)(2,1)} %get-tuple-element.14.rest_0_), channel_id=1, source_target_pairs={{0,3},{1,0},{2,1},{3,2},{4,7},{5,4},{6,5},{7,6},{8,11},{9,8},{10,9... | collective-permute-start | bytes 1572872 | tf_op jit(solution)/shard_map/ppermute | solution.py:217
  31.9 53.4 %collective-permute-start.2 = (bf16[2,528,256]{2,1,0:T(8,128)(2,1)S(1)}, bf16[2,528,256]{2,1,0:T(8,128)(2,1)S(1)}, u32[]{:S(2)}, u32[]{:S(2)}) collective-permute-start(bf16[2,528,256]{2,1,0:T(8,128)(2,1)S(1)} %get-tuple-element.10.rest_0_), channel_id=1, source_target_pairs={{0,3},{1,0},{2,1},{3,2},{4,7},{5,4},{6,5},{7,6},{8,11},{9,8},{10,9... | collective-permute-start | bytes 1622024 | tf_op jit(solution)/shard_map/ppermute | solution.py:217
  35.4 60.5 %collective-permute-start.3 = (bf16[2,2,256,256]{3,2,1,0:T(8,128)(2,1)}, bf16[2,2,256,256]{3,2,1,0:T(8,128)(2,1)}, u32[]{:S(2)}, u32[]{:S(2)}) collective-permute-start(bf16[2,2,256,256]{3,2,1,0:T(8,128)(2,1)} %get-tuple-element.14.rest_0_), channel_id=1, source_target_pairs={{0,1},{1,2},{2,3},{3,0},{4,5},{5,6},{6,7},{7,4},{8,9},{9,10},{10,1... | collective-permute-start | bytes 1572872 | tf_op jit(solution)/shard_map/ppermute | solution.py:217
  45.2 50.6 %collective-permute-start.5 = (bf16[2,2,256,256]{3,2,1,0:T(8,128)(2,1)}, bf16[2,2,256,256]{3,2,1,0:T(8,128)(2,1)}, u32[]{:S(2)}, u32[]{:S(2)}) collective-permute-start(bf16[2,2,256,256]{3,2,1,0:T(8,128)(2,1)} %collective-permute-done.4.rest_3_), channel_id=1, source_target_pairs={{0,3},{1,0},{2,1},{3,2},{4,7},{5,4},{6,5},{7,6},{8,11},{9,8},{10,9... | collective-permute-start | bytes 1572872 | tf_op jit(solution)/shard_map/ppermute | solution.py:217
  50.1 35.2 %collective-permute-start.1 = (bf16[2,528,256]{2,1,0:T(8,128)(2,1)S(1)}, bf16[2,528,256]{2,1,0:T(8,128)(2,1)S(1)}, u32[]{:S(2)}, u32[]{:S(2)}) collective-permute-start(bf16[2,528,256]{2,1,0:T(8,128)(2,1)S(1)} %collective-permute-done.rest_1_), channel_id=1, source_target_pairs={{0,1},{1,2},{2,3},{3,0},{4,5},{5,6},{6,7},{7,4},{8,9},{9,10},{10,1... | collective-permute-start | bytes 1622024 | tf_op jit(solution)/shard_map/ppermute | solution.py:217
  79.0 5.9 %copy-start.3 = (s32[512]{0:T(512)S(1)}, s32[512]{0:T(512)}, u32[]{:S(2)}) copy-start(s32[512]{0:T(512)} %param.10) | copy-start | bytes 6148
  80.6 14.2 %all-to-all-start.1 = ((bf16[4,128,512]{2,1,0:T(8,128)(2,1)}), bf16[4,128,512]{2,1,0:T(8,128)(2,1)S(1)}, u32[]{:S(2)}, u32[]{:S(2)}) async-start(bf16[4,128,512]{2,1,0:T(8,128)(2,1)} %bitcast.26), calls=%async_computation.1 | async-start | bytes 1048576 | tf_op jit(solution)/shard_map/all_to_all | solution.py:302

commit v6 on v5

--- a/solution.py
+++ b/solution.py
@@ -95,7 +95,36 @@
             right_out[t, q] = matmul_nt(right[t, q], order).astype(BF16)
 
 
-def middle_kernel(classes, parts, qcol, *rest):
+def sum_kernel(sec, terms, moved_hbm, rows_in, out, moved, route, sems):
+    parts = sems.shape[0]
+    deep = moved.shape[0] // parts
+    copies = []
+    for i in range(parts):
+        rows = pl.ds(i * deep, deep)
+        copies.append(pltpu.make_async_copy(moved_hbm.at[rows], moved.at[rows], sems.at[i]))
+        copies[-1].start()
+    cols = rows_in[...].astype(F32).T
+    width = out.shape[1] // 2
+    k = iota((1, route.shape[1]), 1)
+    which = (k // sec) % terms
+    sector = (k // (terms * sec)) * sec + k % sec
+    wanted = jnp.broadcast_to(cols[:, 0:1], route.shape)
+    for t in range(1, terms):
+        wanted = jnp.where(which == t, cols[:, t : t + 1], wanted)
+    route[...] = (wanted == sector.astype(F32)).astype(F32).astype(BF16)
+    total = None
+    for i in range(parts):
+        copies[i].wait()
+        at = slice(i * deep, (i + 1) * deep)
+        image = matmul(route[:, at], moved[at, :])
+        total = image if total is None else total + image
+    line = iota((1, out.shape[1]), 1)
+    r = (line >= width).astype(jnp.int32)
+    edge = jnp.maximum(2 * lax.axis_index("blk") + r, line - r * width)
+    out[...] = jnp.where(edge.astype(F32) < cols[:, terms : terms + 1], total, 0.0).astype(BF16)
+
+
+def middle_kernel(classes, spread, parts, qrow, *rest):
     sources, (out, wide) = rest[:-2], rest[-2:]
     each, nsec, width = sources[0].shape[0], parts.shape[1], sources[0].shape[2]
     terms = each * len(sources)
@@ -105,15 +134,19 @@
         total = total + parts[x].astype(F32)
     for j in range(ROWS):
         wide[wide.shape[0] - 1, pl.ds(j, nsec, stride=ROWS), :] = total[:, j * LANES : (j + 1) * LANES]
-    chosen = []
-    for q in range(classes):
-        kept = jnp.where(qcol[...] == q, total, 0.0).astype(BF16)
-        chosen.append(jnp.concatenate([kept[:, :width], kept[:, width:]], axis=0))
+    kept = total.astype(BF16)
+    stacked = jnp.concatenate([kept[:, :width], kept[:, width:]], axis=0)
+    mine = iota((nsec, qrow.shape[1]), 0) * spread + lax.axis_index("term")
+    mine = (mine == iota((nsec, qrow.shape[1]), 1)).astype(F32).astype(BF16)
+    classes_row = jnp.broadcast_to(qrow[...].astype(F32), (8, qrow.shape[1])).astype(BF16)
+    pick = matmul_nt(classes_row, mine)[0:1, :]
+    pick = jnp.concatenate([pick, pick], axis=1)
     for t in range(terms):
         left = sources[t // each]
-        image = matmul_nt(left[t % each, 0:width, :], chosen[0])
+        image = matmul_nt(left[t % each, 0:width, :], stacked)
         for q in range(1, classes):
-            image = image + matmul_nt(left[t % each, q * width : (q + 1) * width, :], chosen[q])
+            other = matmul_nt(left[t % each, q * width : (q + 1) * width, :], stacked)
+            image = jnp.where(pick == float(q), other, image)
         for j in range(4):
             ri, r = j // 2, j % 2
             wide[4 * (t // ROWS) + j, pl.ds(t % ROWS, half, stride=ROWS), :] = image[
@@ -283,35 +316,37 @@
     ].reshape(all_terms, nsec)
     conn_all = conn_all.astype(jnp.int32)
 
-    k = jnp.arange(nblk * pairs, dtype=jnp.int32)
-    k_term = (k // sec) % terms
-    k_sector = (k // pairs) * sec + k % sec
-    wanted = jnp.zeros((nsec, k.shape[0]), jnp.int32)
-    for t in range(terms):
-        wanted = jnp.where(k_term[None, :] == t, by_owner(connect[t])[:, None], wanted)
-    route = (wanted == k_sector[None, :]).astype(BF16)
-    element = jnp.arange(band * width, dtype=jnp.int32)
-    edge = jnp.maximum(blk * band + element // width, element % width)
-    keep = edge[None, :] < by_owner(sector_dims)[:, None]
-    qcol = lax.dynamic_slice_in_dim(by_owner(qclass), x * kept, kept)[:, None]
-
+    rows = jnp.stack([by_owner(connect[t]) for t in range(terms)] + [by_owner(sector_dims)])
+    rows = jnp.pad(rows, ((0, -rows.shape[0] % 8), (0, 0)))
     moved = lax.all_to_all(
         sent.reshape(nblk, pairs, band * width), "blk", split_axis=0, concat_axis=0, tiled=True
     ).reshape(nblk * pairs, band * width)
-    total = jnp.where(keep, matmul(route, moved), 0.0).astype(BF16)
+    moved, lefts, rights, conn_all = lax.optimization_barrier((moved, lefts, rights, conn_all))
+    total = call(
+        functools.partial(sum_kernel, sec, terms),
+        bf16(nsec, band * width),
+        [hbm, vmem],
+        [
+            pltpu.VMEM((nblk * pairs, band * width), BF16),
+            pltpu.VMEM((nsec, nblk * pairs), BF16),
+            pltpu.SemaphoreType.DMA((2,)),
+        ],
+        12 << 20,
+        2 * nsec * nblk * pairs * band * width,
+        moved, rows,
+    )
     parts = lax.all_to_all(
         total.reshape(nterm, kept, band * width), "term", split_axis=0, concat_axis=0, tiled=True
     )
     sent = call(
-        functools.partial(middle_kernel, classes),
+        functools.partial(middle_kernel, classes, sec),
         bf16(nblk, ROWS, slots * LANES),
         [vmem] * (2 + nterm),
         [pltpu.VMEM((slots, nblk * ROWS, LANES), F32)],
         16 << 20,
         2 * all_terms * classes * width**3,
-        parts, qcol, *lefts,
-    )
-    sent, rights, conn_all = lax.optimization_barrier((sent, rights, conn_all))
+        parts, q_row, *lefts,
+    )
     moved = lax.all_to_all(sent, "blk", split_axis=0, concat_axis=0, tiled=True)
     sent = call(
         functools.partial(target_kernel, sec),

time: 187 us -> 188 us (level)
  blocking collectives: 85.5 us -> 99.5 us
  waiting for transfers between devices: 43.3 us -> 33 us
  starting transfers between devices: 43.3 us -> 39 us
  Pallas kernels: 10.9 us -> 13.3 us
    all_to_all x1, waiting for transfers between devices: 26.9 us -> 8.81 us  [on_device(): lax.all_to_all(sent.reshape(nblk, pairs, band * width), 'blk', split_axis...]
    ppermute x6, waiting for transfers between devices: 6.86 us -> 24.1 us  [from_all(): lax.ppermute(v, axis, [(i, (i + d) % n) for i in range(n)])]
    all_to_all x0 -> x1, blocking collectives: none -> 14 us  [on_device(): lax.all_to_all(total.reshape(nterm, kept, band * width), 'term', split_ax...]
    all_to_all x1 -> x0, waiting for transfers between devices: 9.46 us -> none  [on_device(): lax.all_to_all(total.reshape(nterm, kept, band * width), 'term', split_ax...]
    all_to_all x1 -> x0, starting transfers between devices: 4.29 us -> none  [on_device(): lax.all_to_all(total.reshape(nterm, kept, band * width), 'term', split_ax...]
    pallas_call x5 -> x6, Pallas kernels: 10.9 us -> 13.3 us  [call(): pl.pallas_call(kernel, out_shape=out_shape, in_specs=in_specs, out_specs=...]
  transfers between devices with their start and end apart: 8 -> 7, of which waited for: 3 -> 5; matrix products, arithmetic and copies ran while one was open for 1% -> 1% of each run, Pallas kernels for 1% -> 1%
where the time goes in v6:
time: 188 us; the launch traced here: 187 us
  blocking collectives  99.5 us (53%)
  starting transfers between devices  39 us (21%)
  waiting for transfers between devices  33 us (18%)
  Pallas kernels  13.3 us (7%)
    all_to_all x1, blocking collectives, on_device(): moved = lax.all_to_all(sent, 'blk', split_axis=0, concat_axis=0, tiled=True)  67 us
    ppermute x6, waiting for transfers between devices, from_all(): lax.ppermute(v, axis, [(i, (i + d) % n) for i in range(n)])  24.1 us
    ppermute x6, starting transfers between devices, from_all(): lax.ppermute(v, axis, [(i, (i + d) % n) for i in range(n)])  19.7 us
    all_to_all x1, starting transfers between devices, on_device(): lax.all_to_all(sent.reshape(nblk, pairs, band * width), 'blk', split_axis...  19.3 us
    all_to_all x1, blocking collectives, on_device(): lax.all_to_all(sent, 'term', split_axis=0, concat_axis=0, tiled=True)  18.5 us
    all_to_all x1, blocking collectives, on_device(): lax.all_to_all(total.reshape(nterm, kept, band * width), 'term', split_ax...  14 us
    pallas_call x6, Pallas kernels, call(): pl.pallas_call(kernel, out_shape=out_shape, in_specs=in_specs, out_specs=...  13.3 us
    all_to_all x1, waiting for transfers between devices, on_device(): lax.all_to_all(sent.reshape(nblk, pairs, band * width), 'blk', split_axis...  8.81 us
  transfers between devices with their start and end apart: 7, of which 5 were waited for; matrix products, arithmetic and copies ran while one was open for 1% of the time, Pallas kernels for 1%

profile of v6, /device:TPU:32, one launch (start us, length us, event | category | flops | bytes accessed | tf_op | source)
XLA Modules:
  0.0 187.0 jit_solution(16365251430005446485)
XLA Ops:
  0.6 3.5 %shard_map.77 = bf16[1024,512]{1,0:T(8,128)(2,1)} custom-call(bf16[4,256,256]{2,1,0:T(8,128)(2,1)} %psi_hbm.1, bf16[2,2,256,256]{3,2,1,0:T(8,128)(2,1)} %left.1, bf16[2,2,256,256]{3,2,1,0:T(8,128)(2,1)} %right.1, s32[2,512]{1,0:T(2,128)} %conn.1, s32[1,512]{1,0:T(1,128)} %bitcast.17, s32[1,512]{1,0:T(1,128)} %bitcast.20), custom_call_target="tpu_custom_call" | custom-call | flops 671088640 | bytes 6291456 | tf_op jit(solution)/shard_map/pallas_call | solution.py:237
  4.2 0.0 copy-start
  4.2 0.0 copy-start.1
  4.2 0.0 copy-start.2
  4.2 0.0 copy-start.4
  4.2 19.3 %all-to-all-start = ((bf16[128,8,512]{2,1,0:T(8,128)(2,1)}), bf16[128,8,512]{2,1,0:T(8,128)(2,1)S(1)}, u32[]{:S(2)}, u32[]{:S(2)}) async-start(bf16[128,8,512]{2,1,0:T(8,128)(2,1)} %bitcast.22), calls=%async_computation | async-start | bytes 2097152 | tf_op jit(solution)/shard_map/all_to_all | solution.py:321
  23.6 1.2 shard_map.78
  24.8 3.4 %collective-permute-start = (bf16[2,528,256]{2,1,0:T(8,128)(2,1)S(1)}, bf16[2,528,256]{2,1,0:T(8,128)(2,1)S(1)}, u32[]{:S(2)}, u32[]{:S(2)}) collective-permute-start(bf16[2,528,256]{2,1,0:T(8,128)(2,1)S(1)} %get-tuple-element.17.rest_0_), channel_id=1, source_target_pairs={{0,1},{1,2},{2,3},{3,0},{4,5},{5,6},{6,7},{7,4},{8,9},{9,10},{10,1... | collective-permute-start | bytes 1622024 | tf_op jit(solution)/shard_map/ppermute | solution.py:250
  28.2 3.7 %collective-permute-start.4 = (bf16[2,2,256,256]{3,2,1,0:T(8,128)(2,1)}, bf16[2,2,256,256]{3,2,1,0:T(8,128)(2,1)}, u32[]{:S(2)}, u32[]{:S(2)}) collective-permute-start(bf16[2,2,256,256]{3,2,1,0:T(8,128)(2,1)} %get-tuple-element.22.rest_0_), channel_id=1, source_target_pairs={{0,3},{1,0},{2,1},{3,2},{4,7},{5,4},{6,5},{7,6},{8,11},{9,8},{10,9... | collective-permute-start | bytes 1572872 | tf_op jit(solution)/shard_map/ppermute | solution.py:250
  31.9 3.5 %collective-permute-start.2 = (bf16[2,528,256]{2,1,0:T(8,128)(2,1)S(1)}, bf16[2,528,256]{2,1,0:T(8,128)(2,1)S(1)}, u32[]{:S(2)}, u32[]{:S(2)}) collective-permute-start(bf16[2,528,256]{2,1,0:T(8,128)(2,1)S(1)} %get-tuple-element.17.rest_0_), channel_id=1, source_target_pairs={{0,3},{1,0},{2,1},{3,2},{4,7},{5,4},{6,5},{7,6},{8,11},{9,8},{10,9... | collective-permute-start | bytes 1622024 | tf_op jit(solution)/shard_map/ppermute | solution.py:250
  35.3 6.9 %collective-permute-done.rest_1_ = bf16[2,528,256]{2,1,0:T(8,128)(2,1)S(1)} collective-permute-done((bf16[2,528,256]{2,1,0:T(8,128)(2,1)S(1)}, bf16[2,528,256]{2,1,0:T(8,128)(2,1)S(1)}, u32[]{:S(2)}, u32[]{:S(2)}) %collective-permute-start) | collective-permute-done | bytes 540704 | tf_op jit(solution)/shard_map/ppermute | solution.py:250
  42.2 2.2 %collective-permute-start.1 = (bf16[2,528,256]{2,1,0:T(8,128)(2,1)S(1)}, bf16[2,528,256]{2,1,0:T(8,128)(2,1)}, u32[]{:S(2)}, u32[]{:S(2)}) collective-permute-start(bf16[2,528,256]{2,1,0:T(8,128)(2,1)S(1)} %collective-permute-done.rest_1_), channel_id=1, source_target_pairs={{0,1},{1,2},{2,3},{3,0},{4,5},{5,6},{6,7},{7,4},{8,9},{9,10},{10,1... | collective-permute-start | bytes 1622024 | tf_op jit(solution)/shard_map/ppermute | solution.py:250
  44.4 3.4 %collective-permute-start.3 = (bf16[2,2,256,256]{3,2,1,0:T(8,128)(2,1)}, bf16[2,2,256,256]{3,2,1,0:T(8,128)(2,1)}, u32[]{:S(2)}, u32[]{:S(2)}) collective-permute-start(bf16[2,2,256,256]{3,2,1,0:T(8,128)(2,1)} %get-tuple-element.22.rest_0_), channel_id=1, source_target_pairs={{0,1},{1,2},{2,3},{3,0},{4,5},{5,6},{6,7},{7,4},{8,9},{9,10},{10,1... | collective-permute-start | bytes 1572872 | tf_op jit(solution)/shard_map/ppermute | solution.py:250
  47.8 3.7 %collective-permute-start.5 = (bf16[2,2,256,256]{3,2,1,0:T(8,128)(2,1)}, bf16[2,2,256,256]{3,2,1,0:T(8,128)(2,1)}, u32[]{:S(2)}, u32[]{:S(2)}) collective-permute-start(bf16[2,2,256,256]{3,2,1,0:T(8,128)(2,1)} %collective-permute-done.4.rest_3_), channel_id=1, source_target_pairs={{0,3},{1,0},{2,1},{3,2},{4,7},{5,4},{6,5},{7,6},{8,11},{9,8},{10,9... | collective-permute-start | bytes 1572872 | tf_op jit(solution)/shard_map/ppermute | solution.py:250
  51.5 0.1 reshape.24
  51.7 0.1 reshape_squeeze.6
  51.8 0.1 copy.10
  51.8 0.1 reshape_squeeze.7
  52.0 0.1 copy.11
  52.0 0.1 copy.12
  52.2 4.5 %collective-permute-done.2.rest_3_ = bf16[2,528,256]{2,1,0:T(8,128)(2,1)S(1)} collective-permute-done((bf16[2,528,256]{2,1,0:T(8,128)(2,1)S(1)}, bf16[2,528,256]{2,1,0:T(8,128)(2,1)S(1)}, u32[]{:S(2)}, u32[]{:S(2)}) %collective-permute-start.2) | collective-permute-done | bytes 540704 | tf_op jit(solution)/shard_map/ppermute | solution.py:250
  56.7 3.9 %collective-permute-done.1.rest_2_ = bf16[2,528,256]{2,1,0:T(8,128)(2,1)} collective-permute-done((bf16[2,528,256]{2,1,0:T(8,128)(2,1)S(1)}, bf16[2,528,256]{2,1,0:T(8,128)(2,1)}, u32[]{:S(2)}, u32[]{:S(2)}) %collective-permute-start.1) | collective-permute-done | bytes 540704 | tf_op jit(solution)/shard_map/ppermute | solution.py:250
  60.6 0.7 slice.33
  61.4 8.8 %collective-permute-done.3.rest_1_ = bf16[2,2,256,256]{3,2,1,0:T(8,128)(2,1)} collective-permute-done((bf16[2,2,256,256]{3,2,1,0:T(8,128)(2,1)}, bf16[2,2,256,256]{3,2,1,0:T(8,128)(2,1)}, u32[]{:S(2)}, u32[]{:S(2)}) %collective-permute-start.3) | collective-permute-done | bytes 524320 | tf_op jit(solution)/shard_map/ppermute | solution.py:250
  70.2 8.8 %all-to-all-done = bf16[128,8,512]{2,1,0:T(8,128)(2,1)S(1)} async-done(((bf16[128,8,512]{2,1,0:T(8,128)(2,1)}), bf16[128,8,512]{2,1,0:T(8,128)(2,1)S(1)}, u32[]{:S(2)}, u32[]{:S(2)}) %all-to-all-start) | async-done | bytes 1048608 | tf_op jit(solution)/shard_map/all_to_all | solution.py:321
  79.0 1.3 shard_map.79
  80.3 14.0 %all_to_all.20.parts = bf16[4,128,512]{2,1,0:T(8,128)(2,1)S(1)} all-to-all(bf16[4,128,512]{2,1,0:T(8,128)(2,1)S(1)} %bitcast.15), channel_id=1, replica_groups=mesh['blk'=128,'term'=4] {'term'}, dimensions={0} | all-to-all | bytes 1048576 | tf_op jit(solution)/shard_map/all_to_all | solution.py:338
  94.4 2.1 %shard_map.80 = bf16[128,4,1152]{2,1,0:T(4,128)(2,1)S(1)} custom-call(bf16[4,128,512]{2,1,0:T(8,128)(2,1)S(1)} %all_to_all.20.parts, s32[1,512]{1,0:T(1,128)S(1)} %bitcast.18, bf16[2,528,256]{2,1,0:T(8,128)(2,1)S(1)} %get-tuple-element.17.rest_0_, bf16[2,528,256]{2,1,0:T(8,128)(2,1)S(1)} %collective-permute-done.rest_1_, ...), custom_call_target="tpu_custom_call" | custom-call | flops 536870912 | bytes 6291456 | tf_op jit(solution)/shard_map/pallas_call | solution.py:237
  96.5 67.0 %all_to_all.21.moved = bf16[128,4,1152]{2,1,0:T(4,128)(2,1)S(1)} all-to-all(bf16[128,4,1152]{2,1,0:T(4,128)(2,1)S(1)} %shard_map.80), channel_id=1, replica_groups=mesh['blk'=128,'term'=4] {'blk'}, dimensions={0} | all-to-all | bytes 2359296 | tf_op jit(solution)/shard_map/all_to_all | solution.py:350
  163.4 4.0 %shard_map.81 = bf16[4,1024,128]{2,1,0:T(8,128)(2,1)S(1)} custom-call(bf16[128,4,1152]{2,1,0:T(4,128)(2,1)S(1)} %all_to_all.21.moved, s32[8,512]{1,0:T(8,128)S(1)} %bitcast.16, s32[1,512]{1,0:T(1,128)S(1)} %bitcast.19, s32[1,512]{1,0:T(1,128)S(1)} %bitcast.21, bf16[2,2,256,256]{3,2,1,0:T(8,128)(2,1)} %get-tuple-element.22.rest_0_, ...), custom_call_target="tpu_custom_call" | custom-call | flops 1610612736 | bytes 6291456 | tf_op jit(solution)/shard_map/pallas_call | solution.py:237
  167.5 18.5 %all_to_all.22.parts = bf16[4,1024,128]{2,1,0:T(8,128)(2,1)S(1)} all-to-all(bf16[4,1024,128]{2,1,0:T(8,128)(2,1)S(1)} %shard_map.81), channel_id=1, replica_groups=mesh['blk'=128,'term'=4] {'term'}, dimensions={0} | all-to-all | bytes 2097152 | tf_op jit(solution)/shard_map/all_to_all | solution.py:365
  185.9 1.1 shard_map.82
  (16 shorter events, 0.1 us)
Async XLA Ops:
  4.2 19.4 %copy-start = (bf16[2,2,256,256]{3,2,1,0:T(8,128)(2,1)S(1)}, bf16[2,2,256,256]{3,2,1,0:T(8,128)(2,1)}, u32[]{:S(2)}) copy-start(bf16[2,2,256,256]{3,2,1,0:T(8,128)(2,1)} %left.1) | copy-start | bytes 1572868
  4.2 19.4 %copy-start.1 = (bf16[2,2,256,256]{3,2,1,0:T(8,128)(2,1)S(1)}, bf16[2,2,256,256]{3,2,1,0:T(8,128)(2,1)}, u32[]{:S(2)}) copy-start(bf16[2,2,256,256]{3,2,1,0:T(8,128)(2,1)} %right.1) | copy-start | bytes 1572868
  4.2 19.4 %copy-start.2 = (s32[2,512]{1,0:T(2,128)S(1)}, s32[2,512]{1,0:T(2,128)}, u32[]{:S(2)}) copy-start(s32[2,512]{1,0:T(2,128)} %conn.1) | copy-start | bytes 12292
  4.2 47.3 %copy-start.4 = (s32[512]{0:T(512)S(1)}, s32[512]{0:T(512)}, u32[]{:S(2)}) copy-start(s32[512]{0:T(512)} %param.11) | copy-start | bytes 6148
  4.2 74.8 %all-to-all-start = ((bf16[128,8,512]{2,1,0:T(8,128)(2,1)}), bf16[128,8,512]{2,1,0:T(8,128)(2,1)S(1)}, u32[]{:S(2)}, u32[]{:S(2)}) async-start(bf16[128,8,512]{2,1,0:T(8,128)(2,1)} %bitcast.22), calls=%async_computation | async-start | bytes 2097152 | tf_op jit(solution)/shard_map/all_to_all | solution.py:321
  24.8 17.4 %collective-permute-start = (bf16[2,528,256]{2,1,0:T(8,128)(2,1)S(1)}, bf16[2,528,256]{2,1,0:T(8,128)(2,1)S(1)}, u32[]{:S(2)}, u32[]{:S(2)}) collective-permute-start(bf16[2,528,256]{2,1,0:T(8,128)(2,1)S(1)} %get-tuple-element.17.rest_0_), channel_id=1, source_target_pairs={{0,1},{1,2},{2,3},{3,0},{4,5},{5,6},{6,7},{7,4},{8,9},{9,10},{10,1... | collective-permute-start | bytes 1622024 | tf_op jit(solution)/shard_map/ppermute | solution.py:250
  28.2 19.6 %collective-permute-start.4 = (bf16[2,2,256,256]{3,2,1,0:T(8,128)(2,1)}, bf16[2,2,256,256]{3,2,1,0:T(8,128)(2,1)}, u32[]{:S(2)}, u32[]{:S(2)}) collective-permute-start(bf16[2,2,256,256]{3,2,1,0:T(8,128)(2,1)} %get-tuple-element.22.rest_0_), channel_id=1, source_target_pairs={{0,3},{1,0},{2,1},{3,2},{4,7},{5,4},{6,5},{7,6},{8,11},{9,8},{10,9... | collective-permute-start | bytes 1572872 | tf_op jit(solution)/shard_map/ppermute | solution.py:250
  31.9 24.8 %collective-permute-start.2 = (bf16[2,528,256]{2,1,0:T(8,128)(2,1)S(1)}, bf16[2,528,256]{2,1,0:T(8,128)(2,1)S(1)}, u32[]{:S(2)}, u32[]{:S(2)}) collective-permute-start(bf16[2,528,256]{2,1,0:T(8,128)(2,1)S(1)} %get-tuple-element.17.rest_0_), channel_id=1, source_target_pairs={{0,3},{1,0},{2,1},{3,2},{4,7},{5,4},{6,5},{7,6},{8,11},{9,8},{10,9... | collective-permute-start | bytes 1622024 | tf_op jit(solution)/shard_map/ppermute | solution.py:250
  42.2 18.4 %collective-permute-start.1 = (bf16[2,528,256]{2,1,0:T(8,128)(2,1)S(1)}, bf16[2,528,256]{2,1,0:T(8,128)(2,1)}, u32[]{:S(2)}, u32[]{:S(2)}) collective-permute-start(bf16[2,528,256]{2,1,0:T(8,128)(2,1)S(1)} %collective-permute-done.rest_1_), channel_id=1, source_target_pairs={{0,1},{1,2},{2,3},{3,0},{4,5},{5,6},{6,7},{7,4},{8,9},{9,10},{10,1... | collective-permute-start | bytes 1622024 | tf_op jit(solution)/shard_map/ppermute | solution.py:250
  44.4 25.7 %collective-permute-start.3 = (bf16[2,2,256,256]{3,2,1,0:T(8,128)(2,1)}, bf16[2,2,256,256]{3,2,1,0:T(8,128)(2,1)}, u32[]{:S(2)}, u32[]{:S(2)}) collective-permute-start(bf16[2,2,256,256]{3,2,1,0:T(8,128)(2,1)} %get-tuple-element.22.rest_0_), channel_id=1, source_target_pairs={{0,1},{1,2},{2,3},{3,0},{4,5},{5,6},{6,7},{7,4},{8,9},{9,10},{10,1... | collective-permute-start | bytes 1572872 | tf_op jit(solution)/shard_map/ppermute | solution.py:250
  47.8 22.3 %collective-permute-start.5 = (bf16[2,2,256,256]{3,2,1,0:T(8,128)(2,1)}, bf16[2,2,256,256]{3,2,1,0:T(8,128)(2,1)}, u32[]{:S(2)}, u32[]{:S(2)}) collective-permute-start(bf16[2,2,256,256]{3,2,1,0:T(8,128)(2,1)} %collective-permute-done.4.rest_3_), channel_id=1, source_target_pairs={{0,3},{1,0},{2,1},{3,2},{4,7},{5,4},{6,5},{7,6},{8,11},{9,8},{10,9... | collective-permute-start | bytes 1572872 | tf_op jit(solution)/shard_map/ppermute | solution.py:250
  79.0 15.4 %copy-start.3 = (s32[512]{0:T(512)S(1)}, s32[512]{0:T(512)}, u32[]{:S(2)}) copy-start(s32[512]{0:T(512)} %param.10) | copy-start | bytes 6148

commit v7 on v5

--- a/solution.py
+++ b/solution.py
@@ -95,7 +95,7 @@
             right_out[t, q] = matmul_nt(right[t, q], order).astype(BF16)
 
 
-def middle_kernel(classes, parts, qcol, *rest):
+def middle_kernel(classes, spread, parts, qrow, *rest):
     sources, (out, wide) = rest[:-2], rest[-2:]
     each, nsec, width = sources[0].shape[0], parts.shape[1], sources[0].shape[2]
     terms = each * len(sources)
@@ -105,15 +105,19 @@
         total = total + parts[x].astype(F32)
     for j in range(ROWS):
         wide[wide.shape[0] - 1, pl.ds(j, nsec, stride=ROWS), :] = total[:, j * LANES : (j + 1) * LANES]
-    chosen = []
-    for q in range(classes):
-        kept = jnp.where(qcol[...] == q, total, 0.0).astype(BF16)
-        chosen.append(jnp.concatenate([kept[:, :width], kept[:, width:]], axis=0))
+    kept = total.astype(BF16)
+    stacked = jnp.concatenate([kept[:, :width], kept[:, width:]], axis=0)
+    mine = iota((nsec, qrow.shape[1]), 0) * spread + lax.axis_index("term")
+    mine = (mine == iota((nsec, qrow.shape[1]), 1)).astype(F32).astype(BF16)
+    classes_row = jnp.broadcast_to(qrow[...].astype(F32), (8, qrow.shape[1])).astype(BF16)
+    pick = matmul_nt(classes_row, mine)[0:1, :]
+    pick = jnp.concatenate([pick, pick], axis=1)
     for t in range(terms):
         left = sources[t // each]
-        image = matmul_nt(left[t % each, 0:width, :], chosen[0])
+        image = matmul_nt(left[t % each, 0:width, :], stacked)
         for q in range(1, classes):
-            image = image + matmul_nt(left[t % each, q * width : (q + 1) * width, :], chosen[q])
+            other = matmul_nt(left[t % each, q * width : (q + 1) * width, :], stacked)
+            image = jnp.where(pick == float(q), other, image)
         for j in range(4):
             ri, r = j // 2, j % 2
             wide[4 * (t // ROWS) + j, pl.ds(t % ROWS, half, stride=ROWS), :] = image[
@@ -293,25 +297,23 @@
     element = jnp.arange(band * width, dtype=jnp.int32)
     edge = jnp.maximum(blk * band + element // width, element % width)
     keep = edge[None, :] < by_owner(sector_dims)[:, None]
-    qcol = lax.dynamic_slice_in_dim(by_owner(qclass), x * kept, kept)[:, None]
-
     moved = lax.all_to_all(
         sent.reshape(nblk, pairs, band * width), "blk", split_axis=0, concat_axis=0, tiled=True
     ).reshape(nblk * pairs, band * width)
+    moved, lefts, rights, conn_all = lax.optimization_barrier((moved, lefts, rights, conn_all))
     total = jnp.where(keep, matmul(route, moved), 0.0).astype(BF16)
     parts = lax.all_to_all(
         total.reshape(nterm, kept, band * width), "term", split_axis=0, concat_axis=0, tiled=True
     )
     sent = call(
-        functools.partial(middle_kernel, classes),
+        functools.partial(middle_kernel, classes, sec),
         bf16(nblk, ROWS, slots * LANES),
         [vmem] * (2 + nterm),
         [pltpu.VMEM((slots, nblk * ROWS, LANES), F32)],
         16 << 20,
         2 * all_terms * classes * width**3,
-        parts, qcol, *lefts,
-    )
-    sent, rights, conn_all = lax.optimization_barrier((sent, rights, conn_all))
+        parts, q_row, *lefts,
+    )
     moved = lax.all_to_all(sent, "blk", split_axis=0, concat_axis=0, tiled=True)
     sent = call(
         functools.partial(target_kernel, sec),

time: 187 us -> 187 us (level)
  blocking collectives: 85.5 us -> 99.5 us
  waiting for transfers between devices: 43.3 us -> 34.1 us
  starting transfers between devices: 43.3 us -> 39.5 us
    ppermute x6, waiting for transfers between devices: 6.86 us -> 25 us  [from_all(): lax.ppermute(v, axis, [(i, (i + d) % n) for i in range(n)])]
    all_to_all x1, waiting for transfers between devices: 26.9 us -> 9.13 us  [on_device(): lax.all_to_all(sent.reshape(nblk, pairs, band * width), 'blk', split_axis...]
    all_to_all x0 -> x1, blocking collectives: none -> 14 us  [on_device(): lax.all_to_all(total.reshape(nterm, kept, band * width), 'term', split_ax...]
    all_to_all x1 -> x0, waiting for transfers between devices: 9.46 us -> none  [on_device(): lax.all_to_all(total.reshape(nterm, kept, band * width), 'term', split_ax...]
    all_to_all x1 -> x0, starting transfers between devices: 4.29 us -> none  [on_device(): lax.all_to_all(total.reshape(nterm, kept, band * width), 'term', split_ax...]
  transfers between devices with their start and end apart: 8 -> 7, of which waited for: 3 -> 5; matrix products, arithmetic and copies ran while one was open for 1% -> 0% of each run, Pallas kernels for 1% -> 0%
where the time goes in v7:
time: 187 us
  blocking collectives  99.5 us (53%)
  starting transfers between devices  39.5 us (21%)
  waiting for transfers between devices  34.1 us (18%)
  Pallas kernels  10 us (5%)
  matrix products  2 us (1%)
    all_to_all x1, blocking collectives, on_device(): moved = lax.all_to_all(sent, 'blk', split_axis=0, concat_axis=0, tiled=True)  67 us
    ppermute x6, waiting for transfers between devices, from_all(): lax.ppermute(v, axis, [(i, (i + d) % n) for i in range(n)])  25 us
    all_to_all x1, starting transfers between devices, on_device(): lax.all_to_all(sent.reshape(nblk, pairs, band * width), 'blk', split_axis...  19.8 us
    ppermute x6, starting transfers between devices, from_all(): lax.ppermute(v, axis, [(i, (i + d) % n) for i in range(n)])  19.7 us
    all_to_all x1, blocking collectives, on_device(): lax.all_to_all(sent, 'term', split_axis=0, concat_axis=0, tiled=True)  18.5 us
    all_to_all x1, blocking collectives, on_device(): lax.all_to_all(total.reshape(nterm, kept, band * width), 'term', split_ax...  14 us
    pallas_call x5, Pallas kernels, call(): pl.pallas_call(kernel, out_shape=out_shape, in_specs=in_specs, out_specs=...  10 us
    all_to_all x1, waiting for transfers between devices, on_device(): lax.all_to_all(sent.reshape(nblk, pairs, band * width), 'blk', split_axis...  9.13 us
  transfers between devices with their start and end apart: 7, of which 5 were waited for; matrix products, arithmetic and copies ran while one was open for 0% of the time, Pallas kernels for 0%

profile of v7, /device:TPU:32, one launch (start us, length us, event | category | flops | bytes accessed | tf_op | source)
XLA Modules:
  0.0 186.6 jit_solution(10111170634628512078)
XLA Ops:
  0.6 3.6 %shard_map.77 = bf16[1024,512]{1,0:T(8,128)(2,1)} custom-call(bf16[4,256,256]{2,1,0:T(8,128)(2,1)} %psi_hbm.1, bf16[2,2,256,256]{3,2,1,0:T(8,128)(2,1)} %left.1, bf16[2,2,256,256]{3,2,1,0:T(8,128)(2,1)} %right.1, s32[2,512]{1,0:T(2,128)} %conn.1, s32[1,512]{1,0:T(1,128)} %bitcast.16, s32[1,512]{1,0:T(1,128)} %bitcast.19), custom_call_target="tpu_custom_call" | custom-call | flops 671088640 | bytes 6291456 | tf_op jit(solution)/shard_map/pallas_call | solution.py:208
  4.2 0.0 copy-start
  4.2 0.0 copy-start.1
  4.2 0.0 copy-start.2
  4.3 0.0 copy-start.4
  4.3 19.8 %all-to-all-start = ((bf16[128,8,512]{2,1,0:T(8,128)(2,1)}), bf16[128,8,512]{2,1,0:T(8,128)(2,1)}, u32[]{:S(2)}, u32[]{:S(2)}) async-start(bf16[128,8,512]{2,1,0:T(8,128)(2,1)} %bitcast.21), calls=%async_computation | async-start | bytes 2097152 | tf_op jit(solution)/shard_map/all_to_all | solution.py:300
  24.1 0.5 shard_map.78
  24.5 3.4 %collective-permute-start = (bf16[2,528,256]{2,1,0:T(8,128)(2,1)S(1)}, bf16[2,528,256]{2,1,0:T(8,128)(2,1)S(1)}, u32[]{:S(2)}, u32[]{:S(2)}) collective-permute-start(bf16[2,528,256]{2,1,0:T(8,128)(2,1)S(1)} %get-tuple-element.17.rest_0_), channel_id=1, source_target_pairs={{0,1},{1,2},{2,3},{3,0},{4,5},{5,6},{6,7},{7,4},{8,9},{9,10},{10,1... | collective-permute-start | bytes 1622024 | tf_op jit(solution)/shard_map/ppermute | solution.py:221
  27.9 3.7 %collective-permute-start.4 = (bf16[2,2,256,256]{3,2,1,0:T(8,128)(2,1)S(1)}, bf16[2,2,256,256]{3,2,1,0:T(8,128)(2,1)}, u32[]{:S(2)}, u32[]{:S(2)}) collective-permute-start(bf16[2,2,256,256]{3,2,1,0:T(8,128)(2,1)S(1)} %get-tuple-element.22.rest_0_), channel_id=1, source_target_pairs={{0,3},{1,0},{2,1},{3,2},{4,7},{5,4},{6,5},{7,6},{8,11},{9,8},{10,9... | collective-permute-start | bytes 1572872 | tf_op jit(solution)/shard_map/ppermute | solution.py:221
  31.6 3.5 %collective-permute-start.2 = (bf16[2,528,256]{2,1,0:T(8,128)(2,1)S(1)}, bf16[2,528,256]{2,1,0:T(8,128)(2,1)S(1)}, u32[]{:S(2)}, u32[]{:S(2)}) collective-permute-start(bf16[2,528,256]{2,1,0:T(8,128)(2,1)S(1)} %get-tuple-element.17.rest_0_), channel_id=1, source_target_pairs={{0,3},{1,0},{2,1},{3,2},{4,7},{5,4},{6,5},{7,6},{8,11},{9,8},{10,9... | collective-permute-start | bytes 1622024 | tf_op jit(solution)/shard_map/ppermute | solution.py:221
  35.1 6.9 %collective-permute-done.rest_1_ = bf16[2,528,256]{2,1,0:T(8,128)(2,1)S(1)} collective-permute-done((bf16[2,528,256]{2,1,0:T(8,128)(2,1)S(1)}, bf16[2,528,256]{2,1,0:T(8,128)(2,1)S(1)}, u32[]{:S(2)}, u32[]{:S(2)}) %collective-permute-start) | collective-permute-done | bytes 540704 | tf_op jit(solution)/shard_map/ppermute | solution.py:221
  42.0 2.2 %collective-permute-start.1 = (bf16[2,528,256]{2,1,0:T(8,128)(2,1)S(1)}, bf16[2,528,256]{2,1,0:T(8,128)(2,1)S(1)}, u32[]{:S(2)}, u32[]{:S(2)}) collective-permute-start(bf16[2,528,256]{2,1,0:T(8,128)(2,1)S(1)} %collective-permute-done.rest_1_), channel_id=1, source_target_pairs={{0,1},{1,2},{2,3},{3,0},{4,5},{5,6},{6,7},{7,4},{8,9},{9,10},{10,1... | collective-permute-start | bytes 1622024 | tf_op jit(solution)/shard_map/ppermute | solution.py:221
  44.2 3.4 %collective-permute-start.3 = (bf16[2,2,256,256]{3,2,1,0:T(8,128)(2,1)S(1)}, bf16[2,2,256,256]{3,2,1,0:T(8,128)(2,1)}, u32[]{:S(2)}, u32[]{:S(2)}) collective-permute-start(bf16[2,2,256,256]{3,2,1,0:T(8,128)(2,1)S(1)} %get-tuple-element.22.rest_0_), channel_id=1, source_target_pairs={{0,1},{1,2},{2,3},{3,0},{4,5},{5,6},{6,7},{7,4},{8,9},{9,10},{10,1... | collective-permute-start | bytes 1572872 | tf_op jit(solution)/shard_map/ppermute | solution.py:221
  47.6 0.1 reshape.97
  47.7 0.0 collective-permute-done.4.rest_3_
  47.7 3.7 %collective-permute-start.5 = (bf16[2,2,256,256]{3,2,1,0:T(8,128)(2,1)}, bf16[2,2,256,256]{3,2,1,0:T(8,128)(2,1)}, u32[]{:S(2)}, u32[]{:S(2)}) collective-permute-start(bf16[2,2,256,256]{3,2,1,0:T(8,128)(2,1)} %collective-permute-done.4.rest_3_), channel_id=1, source_target_pairs={{0,3},{1,0},{2,1},{3,2},{4,7},{5,4},{6,5},{7,6},{8,11},{9,8},{10,9... | collective-permute-start | bytes 1572872 | tf_op jit(solution)/shard_map/ppermute | solution.py:221
  51.4 0.1 reshape_squeeze.6
  51.5 0.1 copy.9
  51.6 0.1 reshape_squeeze.7
  51.7 0.1 copy.10
  51.8 0.1 copy.8
  51.9 4.3 %collective-permute-done.2.rest_3_ = bf16[2,528,256]{2,1,0:T(8,128)(2,1)S(1)} collective-permute-done((bf16[2,528,256]{2,1,0:T(8,128)(2,1)S(1)}, bf16[2,528,256]{2,1,0:T(8,128)(2,1)S(1)}, u32[]{:S(2)}, u32[]{:S(2)}) %collective-permute-start.2) | collective-permute-done | bytes 540704 | tf_op jit(solution)/shard_map/ppermute | solution.py:221
  56.2 4.0 %collective-permute-done.1.rest_2_ = bf16[2,528,256]{2,1,0:T(8,128)(2,1)S(1)} collective-permute-done((bf16[2,528,256]{2,1,0:T(8,128)(2,1)S(1)}, bf16[2,528,256]{2,1,0:T(8,128)(2,1)S(1)}, u32[]{:S(2)}, u32[]{:S(2)}) %collective-permute-start.1) | collective-permute-done | bytes 540704 | tf_op jit(solution)/shard_map/ppermute | solution.py:221
  60.3 9.7 %collective-permute-done.3.rest_1_ = bf16[2,2,256,256]{3,2,1,0:T(8,128)(2,1)} collective-permute-done((bf16[2,2,256,256]{3,2,1,0:T(8,128)(2,1)S(1)}, bf16[2,2,256,256]{3,2,1,0:T(8,128)(2,1)}, u32[]{:S(2)}, u32[]{:S(2)}) %collective-permute-start.3) | collective-permute-done | bytes 524320 | tf_op jit(solution)/shard_map/ppermute | solution.py:221
  70.0 9.1 %all-to-all-done = bf16[128,8,512]{2,1,0:T(8,128)(2,1)} async-done(((bf16[128,8,512]{2,1,0:T(8,128)(2,1)}), bf16[128,8,512]{2,1,0:T(8,128)(2,1)}, u32[]{:S(2)}, u32[]{:S(2)}) %all-to-all-start) | async-done | bytes 1048608 | tf_op jit(solution)/shard_map/all_to_all | solution.py:300
  79.1 2.0 %fusion.2 = bf16[512,512]{1,0:T(8,128)(2,1)S(1)} fusion(bf16[1024,512]{1,0:T(8,128)(2,1)} %bitcast.9, s32[1024]{0:T(1024)S(1)} %fusion.21, s32[512]{0:T(512)S(1)} %bitcast.27, s32[512]{0:T(512)S(1)} %bitcast.26, pred[1024]{0:T(1024)(128)(4,1)S(1)} %get-tuple-element.28, pred[1024]{0:T(1024)(128)(4,1)S(1)} %get-tuple-element.29, s32[512]{0:T(512)S(1)} %fusion.29, ...), kind=kOutput, calls=%fused_computation.3 | convolution fusion | flops 539230208 | bytes 1587200 | tf_op jit(solution)/shard_map/dot_general | solution.py:19
  81.2 14.0 %all_to_all.20.parts = bf16[4,128,512]{2,1,0:T(8,128)(2,1)S(1)} all-to-all(bf16[4,128,512]{2,1,0:T(8,128)(2,1)S(1)} %bitcast.22), channel_id=1, replica_groups=mesh['blk'=128,'term'=4] {'term'}, dimensions={0} | all-to-all | bytes 1048576 | tf_op jit(solution)/shard_map/all_to_all | solution.py:305
  95.2 1.0 shard_map.79
  96.2 67.0 %all_to_all.21.moved = bf16[128,4,1152]{2,1,0:T(4,128)(2,1)S(1)} all-to-all(bf16[128,4,1152]{2,1,0:T(4,128)(2,1)S(1)} %shard_map.79), channel_id=1, replica_groups=mesh['blk'=128,'term'=4] {'blk'}, dimensions={0} | all-to-all | bytes 2359296 | tf_op jit(solution)/shard_map/all_to_all | solution.py:317
  163.2 3.9 %shard_map.80 = bf16[4,1024,128]{2,1,0:T(8,128)(2,1)S(1)} custom-call(bf16[128,4,1152]{2,1,0:T(4,128)(2,1)S(1)} %all_to_all.21.moved, s32[8,512]{1,0:T(8,128)S(1)} %bitcast.15, s32[1,512]{1,0:T(1,128)S(1)} %bitcast.18, s32[1,512]{1,0:T(1,128)S(1)} %bitcast.20, bf16[2,2,256,256]{3,2,1,0:T(8,128)(2,1)S(1)} %get-tuple-element.22.rest_0_, ...), custom_call_target="tpu_custom_call" | custom-call | flops 1610612736 | bytes 6291456 | tf_op jit(solution)/shard_map/pallas_call | solution.py:208
  167.1 18.5 %all_to_all.22.parts = bf16[4,1024,128]{2,1,0:T(8,128)(2,1)S(1)} all-to-all(bf16[4,1024,128]{2,1,0:T(8,128)(2,1)S(1)} %shard_map.80), channel_id=1, replica_groups=mesh['blk'=128,'term'=4] {'term'}, dimensions={0} | all-to-all | bytes 2097152 | tf_op jit(solution)/shard_map/all_to_all | solution.py:332
  185.6 1.1 shard_map.81
  (17 shorter events, 0.1 us)
Async XLA Ops:
  4.2 19.8 %copy-start = (bf16[2,2,256,256]{3,2,1,0:T(8,128)(2,1)S(1)}, bf16[2,2,256,256]{3,2,1,0:T(8,128)(2,1)}, u32[]{:S(2)}) copy-start(bf16[2,2,256,256]{3,2,1,0:T(8,128)(2,1)} %left.1) | copy-start | bytes 1572868
  4.2 19.8 %copy-start.1 = (bf16[2,2,256,256]{3,2,1,0:T(8,128)(2,1)S(1)}, bf16[2,2,256,256]{3,2,1,0:T(8,128)(2,1)}, u32[]{:S(2)}) copy-start(bf16[2,2,256,256]{3,2,1,0:T(8,128)(2,1)} %right.1) | copy-start | bytes 1572868
  4.2 19.8 %copy-start.2 = (s32[2,512]{1,0:T(2,128)S(1)}, s32[2,512]{1,0:T(2,128)}, u32[]{:S(2)}) copy-start(s32[2,512]{1,0:T(2,128)} %conn.1) | copy-start | bytes 12292
  4.3 43.3 %copy-start.4 = (s32[512]{0:T(512)S(1)}, s32[512]{0:T(512)}, u32[]{:S(2)}) copy-start(s32[512]{0:T(512)} %param.11) | copy-start | bytes 6148
  4.3 74.9 %all-to-all-start = ((bf16[128,8,512]{2,1,0:T(8,128)(2,1)}), bf16[128,8,512]{2,1,0:T(8,128)(2,1)}, u32[]{:S(2)}, u32[]{:S(2)}) async-start(bf16[128,8,512]{2,1,0:T(8,128)(2,1)} %bitcast.21), calls=%async_computation | async-start | bytes 2097152 | tf_op jit(solution)/shard_map/all_to_all | solution.py:300
  24.5 17.4 %collective-permute-start = (bf16[2,528,256]{2,1,0:T(8,128)(2,1)S(1)}, bf16[2,528,256]{2,1,0:T(8,128)(2,1)S(1)}, u32[]{:S(2)}, u32[]{:S(2)}) collective-permute-start(bf16[2,528,256]{2,1,0:T(8,128)(2,1)S(1)} %get-tuple-element.17.rest_0_), channel_id=1, source_target_pairs={{0,1},{1,2},{2,3},{3,0},{4,5},{5,6},{6,7},{7,4},{8,9},{9,10},{10,1... | collective-permute-start | bytes 1622024 | tf_op jit(solution)/shard_map/ppermute | solution.py:221
  27.9 19.8 %collective-permute-start.4 = (bf16[2,2,256,256]{3,2,1,0:T(8,128)(2,1)S(1)}, bf16[2,2,256,256]{3,2,1,0:T(8,128)(2,1)}, u32[]{:S(2)}, u32[]{:S(2)}) collective-permute-start(bf16[2,2,256,256]{3,2,1,0:T(8,128)(2,1)S(1)} %get-tuple-element.22.rest_0_), channel_id=1, source_target_pairs={{0,3},{1,0},{2,1},{3,2},{4,7},{5,4},{6,5},{7,6},{8,11},{9,8},{10,9... | collective-permute-start | bytes 1572872 | tf_op jit(solution)/shard_map/ppermute | solution.py:221
  31.6 24.6 %collective-permute-start.2 = (bf16[2,528,256]{2,1,0:T(8,128)(2,1)S(1)}, bf16[2,528,256]{2,1,0:T(8,128)(2,1)S(1)}, u32[]{:S(2)}, u32[]{:S(2)}) collective-permute-start(bf16[2,528,256]{2,1,0:T(8,128)(2,1)S(1)} %get-tuple-element.17.rest_0_), channel_id=1, source_target_pairs={{0,3},{1,0},{2,1},{3,2},{4,7},{5,4},{6,5},{7,6},{8,11},{9,8},{10,9... | collective-permute-start | bytes 1622024 | tf_op jit(solution)/shard_map/ppermute | solution.py:221
  42.0 18.3 %collective-permute-start.1 = (bf16[2,528,256]{2,1,0:T(8,128)(2,1)S(1)}, bf16[2,528,256]{2,1,0:T(8,128)(2,1)S(1)}, u32[]{:S(2)}, u32[]{:S(2)}) collective-permute-start(bf16[2,528,256]{2,1,0:T(8,128)(2,1)S(1)} %collective-permute-done.rest_1_), channel_id=1, source_target_pairs={{0,1},{1,2},{2,3},{3,0},{4,5},{5,6},{6,7},{7,4},{8,9},{9,10},{10,1... | collective-permute-start | bytes 1622024 | tf_op jit(solution)/shard_map/ppermute | solution.py:221
  44.2 25.9 %collective-permute-start.3 = (bf16[2,2,256,256]{3,2,1,0:T(8,128)(2,1)S(1)}, bf16[2,2,256,256]{3,2,1,0:T(8,128)(2,1)}, u32[]{:S(2)}, u32[]{:S(2)}) collective-permute-start(bf16[2,2,256,256]{3,2,1,0:T(8,128)(2,1)S(1)} %get-tuple-element.22.rest_0_), channel_id=1, source_target_pairs={{0,1},{1,2},{2,3},{3,0},{4,5},{5,6},{6,7},{7,4},{8,9},{9,10},{10,1... | collective-permute-start | bytes 1572872 | tf_op jit(solution)/shard_map/ppermute | solution.py:221
  47.7 22.3 %collective-permute-start.5 = (bf16[2,2,256,256]{3,2,1,0:T(8,128)(2,1)}, bf16[2,2,256,256]{3,2,1,0:T(8,128)(2,1)}, u32[]{:S(2)}, u32[]{:S(2)}) collective-permute-start(bf16[2,2,256,256]{3,2,1,0:T(8,128)(2,1)} %collective-permute-done.4.rest_3_), channel_id=1, source_target_pairs={{0,3},{1,0},{2,1},{3,2},{4,7},{5,4},{6,5},{7,6},{8,11},{9,8},{10,9... | collective-permute-start | bytes 1572872 | tf_op jit(solution)/shard_map/ppermute | solution.py:221
  79.1 16.1 %copy-start.3 = (s32[512]{0:T(512)S(1)}, s32[512]{0:T(512)}, u32[]{:S(2)}) copy-start(s32[512]{0:T(512)} %param.10) | copy-start | bytes 6148
